TPU v7x, 256 devices: a whole 4x4x8 slice. The times are simulated.
256 devices in a mesh: tm: 2 (over x_hi), sx: 2 (over core), sy: 64 (over z, y, x_lo).
Axes of the slice: x: 4 (x_hi: 2, x_lo: 2; x = x_hi * 2 + x_lo), y: 4, z: 8, core: 2. Of those that a mesh axis runs over, the one named last changes fastest.
Arguments:
- u_init: float32 [128, 8192], P(None, 'sy'), may hold values from -6 to 6
- guess: float32 [16, 128, 8192], P(('tm', 'sx'), None, 'sy'), may hold values from -6 to 6
- forcing: float32 [64, 128, 8192], P(('tm', 'sx'), None, 'sy'), may hold values from -1.5 to 1.5
- speed_x: float32 [128, 8192], P(None, 'sy'), may hold values from -0.015 to 0.015
- speed_y: float32 [128, 8192], P(None, 'sy'), may hold values from -0.015 to 0.015
- diffusion: float32 [128, 8192], P(None, 'sy'), may hold values from 0.001 to 0.006
Outputs:
- solution: float32 [64, 128, 8192], P(('tm', 'sx'), None, 'sy')
All inputs are finite; a program needn't handle non-finite values.
Results may differ from a plain program's by a relative error of at most 0.00002.
Values sent between devices are 32-bit elements; how exact they have to be, the bound alone decides.
A program may use at most 64 MiB of HBM per device.

v0:
```python
import jax
import jax.numpy as jnp
from jax import lax
from jax.sharding import PartitionSpec as P


def extended(block, sides, width):
    for axis, dim in sides:
        count = lax.axis_size(axis)
        forward = [(i, i + 1) for i in range(count - 1)]
        backward = [(target, source) for source, target in forward]
        low = lax.ppermute(
            lax.slice_in_dim(block, block.shape[dim] - width, None, axis=dim), axis, forward
        )
        high = lax.ppermute(lax.slice_in_dim(block, 0, width, axis=dim), axis, backward)
        block = jnp.concatenate([low, block, high], axis=dim)
    return block


def from_behind(x, axis, by):
    count = lax.axis_size(axis)
    pairs = [(i, i + by) for i in range(count) if 0 <= i + by < count]
    return lax.ppermute(x, axis, pairs)


def slope(padded, coefficients):
    speed_x, speed_y, diffusion = coefficients
    centre = padded[..., 1:-1, 1:-1]
    west_cell = padded[..., :-2, 1:-1]
    east_cell = padded[..., 2:, 1:-1]
    south_cell = padded[..., 1:-1, :-2]
    north_cell = padded[..., 1:-1, 2:]
    along_x = jnp.maximum(speed_x, 0.0) * (centre - west_cell) + jnp.minimum(speed_x, 0.0) * (
        east_cell - centre
    )
    along_y = jnp.maximum(speed_y, 0.0) * (centre - south_cell) + jnp.minimum(speed_y, 0.0) * (
        north_cell - centre
    )
    return (
        -along_x
        - along_y
        + diffusion * (west_cell + east_cell + south_cell + north_cell - 4.0 * centre)
    )


def pad_rows(field, width):
    spec = [(0, 0)] * (field.ndim - 2) + [(width, width), (0, 0)]
    return jnp.pad(field, spec)


def rimmed(field):
    sided = extended(field, (("sy", 2),), 1)
    return pad_rows(sided, 1)


def local(u_init, guess, forcing, speed_x, speed_y, diffusion):
    steps, rows, cols = forcing.shape
    coefficients = (speed_x, speed_y, diffusion)

    def advance(state, factor):
        first = slope(rimmed(state), coefficients)
        middle = state + factor * first
        second = slope(rimmed(middle), coefficients)
        return state + 0.5 * factor * (first + second)

    def single(state, factor):
        return advance(state[None], factor)[0]

    blocks = forcing.reshape(steps // 4, 4, rows, cols)
    place = lax.axis_index(("tm", "sx"))
    received = from_behind(guess[-1], ("tm", "sx"), 1)
    start = jnp.where(place == 0, u_init, received)

    def relax_fine(first_start, c_points):
        starts = jnp.concatenate([first_start[None], c_points[:-1]], 0)
        first_f = advance(starts, 1.0) + blocks[:, 0]
        second_f = advance(first_f, 1.0) + blocks[:, 1]
        third_f = advance(second_f, 1.0) + blocks[:, 2]
        return (first_f, second_f, third_f)

    first_f, second_f, third_f = relax_fine(start, guess)
    resid = blocks[:, 3] + advance(third_f, 1.0) - guess
    lev_b = single(resid[0], 4.0) + resid[1]
    lev_c = single(lev_b, 4.0) + resid[2]
    coarse_rhs = resid[3] + single(lev_c, 4.0)
    zero_state = jnp.zeros_like(coarse_rhs)

    def turn(count, previous):
        candidate = single(previous, 16.0) + coarse_rhs
        return from_behind(candidate, ("tm", "sx"), 1)

    before = lax.fori_loop(0, lax.axis_size(("tm", "sx")) - 1, turn, zero_state)
    own = single(before, 16.0) + coarse_rhs
    cor_a = single(before, 4.0) + resid[0]
    cor_b = single(cor_a, 4.0) + resid[1]
    cor_c = single(cor_b, 4.0) + resid[2]
    corrections = jnp.stack([cor_a, cor_b, cor_c, own], 0)
    corrected = guess + corrections
    start_new = start + before
    fine_a, fine_b, fine_c = relax_fine(start_new, corrected)
    return jnp.stack([fine_a, fine_b, fine_c, corrected], 1).reshape(steps, rows, cols)


def solution(mesh):
    placed = (
        P(None, "sy"),
        P(("tm", "sx"), None, "sy"),
        P(("tm", "sx"), None, "sy"),
        P(None, "sy"),
        P(None, "sy"),
        P(None, "sy"),
    )
    return jax.shard_map(
        local, mesh=mesh, in_specs=placed, out_specs=P(("tm", "sx"), None, "sy"), check_vma=False
    )
```

profile of v0, /device:TPU:132, one launch (start us, length us, event | category | flops | bytes accessed | tf_op | source)
XLA Modules:
  0.0 552.3 jit_solution(15035362823362489936)
XLA Ops:
  3.8 4.2 collective-permute-done.5
  8.1 3.1 collective-permute-start.6
  11.2 7.0 %collective-permute-start.7 = (f32[4,128,1]{2,1,0:T(8,128)S(1)}, f32[4,128,1]{2,1,0:T(8,128)S(1)}, u32[]{:S(2)}, u32[]{:S(2)}) collective-permute-start(f32[4,128,1]{2,1,0:T(8,128)S(1)} %get-tuple-element.134), channel_id=1, source_target_pairs={{1,0},{2,1},{3,2},{4,3},{5,4},{6,5},{7,6},{8,7},{9,8},{10,9},{11,1... | collective-permute-start | bytes 6152 | tf_op jit(solution)/shard_map/ppermute | solution.py:15
  18.2 2.5 collective-permute-done.6
  23.0 2.6 collective-permute-start.8
  25.6 8.1 %collective-permute-start.9 = (f32[4,128,1]{2,1,0:T(8,128)S(1)}, f32[4,128,1]{2,1,0:T(8,128)S(1)}, u32[]{:S(2)}, u32[]{:S(2)}) collective-permute-start(f32[4,128,1]{2,1,0:T(8,128)S(1)} %get-tuple-element.132), channel_id=1, source_target_pairs={{1,0},{2,1},{3,2},{4,3},{5,4},{6,5},{7,6},{8,7},{9,8},{10,9},{11,1... | collective-permute-start | bytes 6152 | tf_op jit(solution)/shard_map/ppermute | solution.py:15
  33.7 2.5 collective-permute-done.8
  38.4 8.7 %collective-permute-start.11 = (f32[4,128,1]{2,1,0:T(8,128)S(1)}, f32[4,128,1]{2,1,0:T(8,128)S(1)}, u32[]{:S(2)}, u32[]{:S(2)}) collective-permute-start(f32[4,128,1]{2,1,0:T(8,128)S(1)} %get-tuple-element.129), channel_id=1, source_target_pairs={{1,0},{2,1},{3,2},{4,3},{5,4},{6,5},{7,6},{8,7},{9,8},{10,9},{11,1... | collective-permute-start | bytes 6152 | tf_op jit(solution)/shard_map/ppermute | solution.py:15
  51.1 8.7 %collective-permute-done.10 = f32[4,128,1]{2,1,0:T(8,128)S(1)} collective-permute-done((f32[4,128,1]{2,1,0:T(8,128)S(1)}, f32[4,128,1]{2,1,0:T(8,128)S(1)}, u32[]{:S(2)}, u32[]{:S(2)}) %collective-permute-start.10) | collective-permute-done | bytes 2080 | tf_op jit(solution)/shard_map/ppermute | solution.py:12
  62.5 8.1 %collective-permute-start.13 = (f32[4,128,1]{2,1,0:T(8,128)S(1)}, f32[4,128,1]{2,1,0:T(8,128)S(1)}, u32[]{:S(2)}, u32[]{:S(2)}) collective-permute-start(f32[4,128,1]{2,1,0:T(8,128)S(1)} %get-tuple-element.128), channel_id=1, source_target_pairs={{1,0},{2,1},{3,2},{4,3},{5,4},{6,5},{7,6},{8,7},{9,8},{10,9},{11,1... | collective-permute-start | bytes 6152 | tf_op jit(solution)/shard_map/ppermute | solution.py:15
  70.7 2.5 collective-permute-done.12
  75.7 8.6 %collective-permute-start.15 = (f32[4,128,1]{2,1,0:T(8,128)S(1)}, f32[4,128,1]{2,1,0:T(8,128)S(1)}, u32[]{:S(2)}, u32[]{:S(2)}) collective-permute-start(f32[4,128,1]{2,1,0:T(8,128)S(1)} %get-tuple-element.125), channel_id=1, source_target_pairs={{1,0},{2,1},{3,2},{4,3},{5,4},{6,5},{7,6},{8,7},{9,8},{10,9},{11,1... | collective-permute-start | bytes 6152 | tf_op jit(solution)/shard_map/ppermute | solution.py:15
  88.2 10.1 %collective-permute-done.14 = f32[4,128,1]{2,1,0:T(8,128)S(1)} collective-permute-done((f32[4,128,1]{2,1,0:T(8,128)S(1)}, f32[4,128,1]{2,1,0:T(8,128)S(1)}, u32[]{:S(2)}, u32[]{:S(2)}) %collective-permute-start.14) | collective-permute-done | bytes 2080 | tf_op jit(solution)/shard_map/ppermute | solution.py:12
  101.1 8.1 %collective-permute-start.17 = (f32[4,128,1]{2,1,0:T(8,128)S(1)}, f32[4,128,1]{2,1,0:T(8,128)S(1)}, u32[]{:S(2)}, u32[]{:S(2)}) collective-permute-start(f32[4,128,1]{2,1,0:T(8,128)S(1)} %get-tuple-element.124), channel_id=1, source_target_pairs={{1,0},{2,1},{3,2},{4,3},{5,4},{6,5},{7,6},{8,7},{9,8},{10,9},{11,1... | collective-permute-start | bytes 6152 | tf_op jit(solution)/shard_map/ppermute | solution.py:15
  109.3 2.4 collective-permute-done.16
  111.7 3.1 collective-permute-done.17
  115.9 8.7 %collective-permute-start.19 = (f32[4,128,1]{2,1,0:T(8,128)S(1)}, f32[4,128,1]{2,1,0:T(8,128)S(1)}, u32[]{:S(2)}, u32[]{:S(2)}) collective-permute-start(f32[4,128,1]{2,1,0:T(8,128)S(1)} %get-tuple-element.121), channel_id=1, source_target_pairs={{1,0},{2,1},{3,2},{4,3},{5,4},{6,5},{7,6},{8,7},{9,8},{10,9},{11,1... | collective-permute-start | bytes 6152 | tf_op jit(solution)/shard_map/ppermute | solution.py:15
  128.5 8.7 %collective-permute-done.18 = f32[4,128,1]{2,1,0:T(8,128)S(1)} collective-permute-done((f32[4,128,1]{2,1,0:T(8,128)S(1)}, f32[4,128,1]{2,1,0:T(8,128)S(1)}, u32[]{:S(2)}, u32[]{:S(2)}) %collective-permute-start.18) | collective-permute-done | bytes 2080 | tf_op jit(solution)/shard_map/ppermute | solution.py:12
  140.0 8.3 %collective-permute-start.21 = (f32[4,128,1]{2,1,0:T(8,128)S(1)}, f32[4,128,1]{2,1,0:T(8,128)S(1)}, u32[]{:S(2)}, u32[]{:S(2)}) collective-permute-start(f32[4,128,1]{2,1,0:T(8,128)S(1)} %get-tuple-element.120), channel_id=1, source_target_pairs={{1,0},{2,1},{3,2},{4,3},{5,4},{6,5},{7,6},{8,7},{9,8},{10,9},{11,1... | collective-permute-start | bytes 6152 | tf_op jit(solution)/shard_map/ppermute | solution.py:15
  153.3 8.6 %collective-permute-start.23 = (f32[1,128,1]{2,1,0:T(8,128)S(1)}, f32[1,128,1]{2,1,0:T(8,128)S(1)}, u32[]{:S(2)}, u32[]{:S(2)}) collective-permute-start(f32[1,128,1]{2,1,0:T(8,128)S(1)} %get-tuple-element.117), channel_id=1, source_target_pairs={{1,0},{2,1},{3,2},{4,3},{5,4},{6,5},{7,6},{8,7},{9,8},{10,9},{11,1... | collective-permute-start | bytes 1544 | tf_op jit(solution)/shard_map/ppermute | solution.py:15
  164.1 8.1 %collective-permute-done.22 = f32[1,128,1]{2,1,0:T(8,128)S(1)} collective-permute-done((f32[1,128,1]{2,1,0:T(8,128)S(1)}, f32[1,128,1]{2,1,0:T(8,128)S(1)}, u32[]{:S(2)}, u32[]{:S(2)}) %collective-permute-start.22) | collective-permute-done | bytes 544 | tf_op jit(solution)/shard_map/ppermute | solution.py:12
  174.6 8.1 %collective-permute-start.25 = (f32[1,128,1]{2,1,0:T(8,128)S(1)}, f32[1,128,1]{2,1,0:T(8,128)S(1)}, u32[]{:S(2)}, u32[]{:S(2)}) collective-permute-start(f32[1,128,1]{2,1,0:T(8,128)S(1)} %get-tuple-element.160), channel_id=1, source_target_pairs={{1,0},{2,1},{3,2},{4,3},{5,4},{6,5},{7,6},{8,7},{9,8},{10,9},{11,1... | collective-permute-start | bytes 1544 | tf_op jit(solution)/shard_map/ppermute | solution.py:15
  185.0 8.5 %collective-permute-start.27 = (f32[1,128,1]{2,1,0:T(8,128)S(1)}, f32[1,128,1]{2,1,0:T(8,128)S(1)}, u32[]{:S(2)}, u32[]{:S(2)}) collective-permute-start(f32[1,128,1]{2,1,0:T(8,128)S(1)} %get-tuple-element.157), channel_id=1, source_target_pairs={{1,0},{2,1},{3,2},{4,3},{5,4},{6,5},{7,6},{8,7},{9,8},{10,9},{11,1... | collective-permute-start | bytes 1544 | tf_op jit(solution)/shard_map/ppermute | solution.py:15
  195.5 8.4 %collective-permute-done.26 = f32[1,128,1]{2,1,0:T(8,128)S(1)} collective-permute-done((f32[1,128,1]{2,1,0:T(8,128)S(1)}, f32[1,128,1]{2,1,0:T(8,128)S(1)}, u32[]{:S(2)}, u32[]{:S(2)}) %collective-permute-start.26) | collective-permute-done | bytes 544 | tf_op jit(solution)/shard_map/ppermute | solution.py:12
  206.2 8.1 %collective-permute-start.29 = (f32[1,128,1]{2,1,0:T(8,128)S(1)}, f32[1,128,1]{2,1,0:T(8,128)S(1)}, u32[]{:S(2)}, u32[]{:S(2)}) collective-permute-start(f32[1,128,1]{2,1,0:T(8,128)S(1)} %get-tuple-element.156), channel_id=1, source_target_pairs={{1,0},{2,1},{3,2},{4,3},{5,4},{6,5},{7,6},{8,7},{9,8},{10,9},{11,1... | collective-permute-start | bytes 1544 | tf_op jit(solution)/shard_map/ppermute | solution.py:15
  216.7 8.5 %collective-permute-start.31 = (f32[1,128,1]{2,1,0:T(8,128)S(1)}, f32[1,128,1]{2,1,0:T(8,128)S(1)}, u32[]{:S(2)}, u32[]{:S(2)}) collective-permute-start(f32[1,128,1]{2,1,0:T(8,128)S(1)} %get-tuple-element.153), channel_id=1, source_target_pairs={{1,0},{2,1},{3,2},{4,3},{5,4},{6,5},{7,6},{8,7},{9,8},{10,9},{11,1... | collective-permute-start | bytes 1544 | tf_op jit(solution)/shard_map/ppermute | solution.py:15
  227.2 8.4 %collective-permute-done.30 = f32[1,128,1]{2,1,0:T(8,128)S(1)} collective-permute-done((f32[1,128,1]{2,1,0:T(8,128)S(1)}, f32[1,128,1]{2,1,0:T(8,128)S(1)}, u32[]{:S(2)}, u32[]{:S(2)}) %collective-permute-start.30) | collective-permute-done | bytes 544 | tf_op jit(solution)/shard_map/ppermute | solution.py:12
  237.9 8.3 %collective-permute-start.33 = (f32[1,128,1]{2,1,0:T(8,128)S(1)}, f32[1,128,1]{2,1,0:T(8,128)S(1)}, u32[]{:S(2)}, u32[]{:S(2)}) collective-permute-start(f32[1,128,1]{2,1,0:T(8,128)S(1)} %get-tuple-element.152), channel_id=1, source_target_pairs={{1,0},{2,1},{3,2},{4,3},{5,4},{6,5},{7,6},{8,7},{9,8},{10,9},{11,1... | collective-permute-start | bytes 1544 | tf_op jit(solution)/shard_map/ppermute | solution.py:15
  248.3 104.3 %while.12 = (s32[]{:T(128)}, f32[128,128]{1,0:T(8,128)S(1)}, f32[128,128]{1,0:T(8,128)S(1)}, f32[128,128]{1,0:T(8,128)S(1)}, f32[128,128]{1,0:T(8,128)S(1)}, /*index=5*/f32[128,128]{1,0:T(8,128)S(1)}, s32[]{:T(128)}) while((s32[]{:T(128)}, f32[128,128]{1,0:T(8,128)S(1)}, f32[128,128]{1,0:T(8,128)S(1)}, f32[128,128]{1,0:T(8,128)S(1)}, ...), condition=%wide.region_1.2_spmd, body=%wide.region_0.1_spmd.sunk | while | flops 1531970 | bytes 1856821 | solution.py:92
  248.4 8.5 %collective-permute-start = (f32[1,128,1]{2,1,0:T(8,128)S(1)}, f32[1,128,1]{2,1,0:T(8,128)S(1)}, u32[]{:S(2)}, u32[]{:S(2)}) collective-permute-start(f32[1,128,1]{2,1,0:T(8,128)S(1)} %get-tuple-element.208), channel_id=1, source_target_pairs={{1,0},{2,1},{3,2},{4,3},{5,4},{6,5},{7,6},{8,7},{9,8},{10,9},{11,1... | collective-permute-start | bytes 1544 | tf_op jit(solution)/shard_map/while/body/eval_jaxpr/ppermute | solution.py:15
  258.8 8.4 %collective-permute-done.1 = f32[1,128,1]{2,1,0:T(8,128)S(1)} collective-permute-done((f32[1,128,1]{2,1,0:T(8,128)S(1)}, f32[1,128,1]{2,1,0:T(8,128)S(1)}, u32[]{:S(2)}, u32[]{:S(2)}) %collective-permute-start.1) | collective-permute-done | bytes 544 | tf_op jit(solution)/shard_map/while/body/eval_jaxpr/ppermute | solution.py:12
  269.6 3.9 collective-permute-start.3
  273.8 6.1 %collective-permute-done.3 = f32[1,128,1]{2,1,0:T(8,128)S(1)} collective-permute-done((f32[1,128,1]{2,1,0:T(8,128)S(1)}, f32[1,128,1]{2,1,0:T(8,128)S(1)}, u32[]{:S(2)}, u32[]{:S(2)}) %collective-permute-start.3) | collective-permute-done | bytes 544 | tf_op jit(solution)/shard_map/while/body/eval_jaxpr/ppermute | solution.py:12
  282.3 5.2 collective-permute-done.4
  289.5 3.9 collective-permute-start.1
  293.7 6.2 %collective-permute-done.1 = f32[1,128,1]{2,1,0:T(8,128)S(1)} collective-permute-done((f32[1,128,1]{2,1,0:T(8,128)S(1)}, f32[1,128,1]{2,1,0:T(8,128)S(1)}, u32[]{:S(2)}, u32[]{:S(2)}) %collective-permute-start.1) | collective-permute-done | bytes 544 | tf_op jit(solution)/shard_map/while/body/eval_jaxpr/ppermute | solution.py:12
  302.2 3.9 collective-permute-start.3
  306.4 6.1 %collective-permute-done.3 = f32[1,128,1]{2,1,0:T(8,128)S(1)} collective-permute-done((f32[1,128,1]{2,1,0:T(8,128)S(1)}, f32[1,128,1]{2,1,0:T(8,128)S(1)}, u32[]{:S(2)}, u32[]{:S(2)}) %collective-permute-start.3) | collective-permute-done | bytes 544 | tf_op jit(solution)/shard_map/while/body/eval_jaxpr/ppermute | solution.py:12
  314.9 5.2 collective-permute-done.4
  322.0 3.9 collective-permute-start.1
  326.3 6.1 %collective-permute-done.1 = f32[1,128,1]{2,1,0:T(8,128)S(1)} collective-permute-done((f32[1,128,1]{2,1,0:T(8,128)S(1)}, f32[1,128,1]{2,1,0:T(8,128)S(1)}, u32[]{:S(2)}, u32[]{:S(2)}) %collective-permute-start.1) | collective-permute-done | bytes 544 | tf_op jit(solution)/shard_map/while/body/eval_jaxpr/ppermute | solution.py:12
  334.7 3.9 collective-permute-start.3
  339.0 6.2 %collective-permute-done.3 = f32[1,128,1]{2,1,0:T(8,128)S(1)} collective-permute-done((f32[1,128,1]{2,1,0:T(8,128)S(1)}, f32[1,128,1]{2,1,0:T(8,128)S(1)}, u32[]{:S(2)}, u32[]{:S(2)}) %collective-permute-start.3) | collective-permute-done | bytes 544 | tf_op jit(solution)/shard_map/while/body/eval_jaxpr/ppermute | solution.py:12
  347.4 5.2 collective-permute-done.4
  354.6 8.1 %collective-permute-start.35 = (f32[1,128,1]{2,1,0:T(8,128)S(1)}, f32[1,128,1]{2,1,0:T(8,128)S(1)}, u32[]{:S(2)}, u32[]{:S(2)}) collective-permute-start(f32[1,128,1]{2,1,0:T(8,128)S(1)} %get-tuple-element.150), channel_id=1, source_target_pairs={{1,0},{2,1},{3,2},{4,3},{5,4},{6,5},{7,6},{8,7},{9,8},{10,9},{11,1... | collective-permute-start | bytes 1544 | tf_op jit(solution)/shard_map/ppermute | solution.py:15
  366.9 8.6 %collective-permute-start.37 = (f32[1,128,1]{2,1,0:T(8,128)S(1)}, f32[1,128,1]{2,1,0:T(8,128)S(1)}, u32[]{:S(2)}, u32[]{:S(2)}) collective-permute-start(f32[1,128,1]{2,1,0:T(8,128)S(1)} %get-tuple-element.146), channel_id=1, source_target_pairs={{1,0},{2,1},{3,2},{4,3},{5,4},{6,5},{7,6},{8,7},{9,8},{10,9},{11,1... | collective-permute-start | bytes 1544 | tf_op jit(solution)/shard_map/ppermute | solution.py:15
  377.8 8.5 %collective-permute-start.39 = (f32[1,128,1]{2,1,0:T(8,128)S(1)}, f32[1,128,1]{2,1,0:T(8,128)S(1)}, u32[]{:S(2)}, u32[]{:S(2)}) collective-permute-start(f32[1,128,1]{2,1,0:T(8,128)S(1)} %get-tuple-element.143), channel_id=1, source_target_pairs={{1,0},{2,1},{3,2},{4,3},{5,4},{6,5},{7,6},{8,7},{9,8},{10,9},{11,1... | collective-permute-start | bytes 1544 | tf_op jit(solution)/shard_map/ppermute | solution.py:15
  388.2 8.4 %collective-permute-done.38 = f32[1,128,1]{2,1,0:T(8,128)S(1)} collective-permute-done((f32[1,128,1]{2,1,0:T(8,128)S(1)}, f32[1,128,1]{2,1,0:T(8,128)S(1)}, u32[]{:S(2)}, u32[]{:S(2)}) %collective-permute-start.38) | collective-permute-done | bytes 544 | tf_op jit(solution)/shard_map/ppermute | solution.py:12
  398.9 8.1 %collective-permute-start.41 = (f32[1,128,1]{2,1,0:T(8,128)S(1)}, f32[1,128,1]{2,1,0:T(8,128)S(1)}, u32[]{:S(2)}, u32[]{:S(2)}) collective-permute-start(f32[1,128,1]{2,1,0:T(8,128)S(1)} %get-tuple-element.142), channel_id=1, source_target_pairs={{1,0},{2,1},{3,2},{4,3},{5,4},{6,5},{7,6},{8,7},{9,8},{10,9},{11,1... | collective-permute-start | bytes 1544 | tf_op jit(solution)/shard_map/ppermute | solution.py:15
  409.1 8.1 %collective-permute-start.47 = (f32[1,128,1]{2,1,0:T(8,128)S(1)}, f32[1,128,1]{2,1,0:T(8,128)S(1)}, u32[]{:S(2)}, u32[]{:S(2)}) collective-permute-start(f32[1,128,1]{2,1,0:T(8,128)S(1)} %get-tuple-element.148), channel_id=1, source_target_pairs={{1,0},{2,1},{3,2},{4,3},{5,4},{6,5},{7,6},{8,7},{9,8},{10,9},{11,1... | collective-permute-start | bytes 1544 | tf_op jit(solution)/shard_map/ppermute | solution.py:15
  419.6 3.9 collective-permute-start.42
  423.9 6.4 %collective-permute-done.42 = f32[1,128,1]{2,1,0:T(8,128)S(1)} collective-permute-done((f32[1,128,1]{2,1,0:T(8,128)S(1)}, f32[1,128,1]{2,1,0:T(8,128)S(1)}, u32[]{:S(2)}, u32[]{:S(2)}) %collective-permute-start.42) | collective-permute-done | bytes 544 | tf_op jit(solution)/shard_map/ppermute | solution.py:12
  432.6 8.1 %collective-permute-start.45 = (f32[1,128,1]{2,1,0:T(8,128)S(1)}, f32[1,128,1]{2,1,0:T(8,128)S(1)}, u32[]{:S(2)}, u32[]{:S(2)}) collective-permute-start(f32[1,128,1]{2,1,0:T(8,128)S(1)} %get-tuple-element.138), channel_id=1, source_target_pairs={{1,0},{2,1},{3,2},{4,3},{5,4},{6,5},{7,6},{8,7},{9,8},{10,9},{11,1... | collective-permute-start | bytes 1544 | tf_op jit(solution)/shard_map/ppermute | solution.py:15
  445.6 8.7 %collective-permute-start.49 = (f32[4,128,1]{2,1,0:T(8,128)S(1)}, f32[4,128,1]{2,1,0:T(8,128)S(1)}, u32[]{:S(2)}, u32[]{:S(2)}) collective-permute-start(f32[4,128,1]{2,1,0:T(8,128)S(1)} %get-tuple-element.116), channel_id=1, source_target_pairs={{1,0},{2,1},{3,2},{4,3},{5,4},{6,5},{7,6},{8,7},{9,8},{10,9},{11,1... | collective-permute-start | bytes 6152 | tf_op jit(solution)/shard_map/ppermute | solution.py:15
  454.3 3.5 collective-permute-done.48
  462.6 8.4 %collective-permute-start.51 = (f32[4,128,1]{2,1,0:T(8,128)S(1)}, f32[4,128,1]{2,1,0:T(8,128)S(1)}, u32[]{:S(2)}, u32[]{:S(2)}) collective-permute-start(f32[4,128,1]{2,1,0:T(8,128)S(1)} %get-tuple-element.114), channel_id=1, source_target_pairs={{1,0},{2,1},{3,2},{4,3},{5,4},{6,5},{7,6},{8,7},{9,8},{10,9},{11,1... | collective-permute-start | bytes 6152 | tf_op jit(solution)/shard_map/ppermute | solution.py:15
  473.4 2.6 collective-permute-done.51
  476.9 8.7 %collective-permute-start.53 = (f32[4,128,1]{2,1,0:T(8,128)S(1)}, f32[4,128,1]{2,1,0:T(8,128)S(1)}, u32[]{:S(2)}, u32[]{:S(2)}) collective-permute-start(f32[4,128,1]{2,1,0:T(8,128)S(1)} %get-tuple-element.111), channel_id=1, source_target_pairs={{1,0},{2,1},{3,2},{4,3},{5,4},{6,5},{7,6},{8,7},{9,8},{10,9},{11,1... | collective-permute-start | bytes 6152 | tf_op jit(solution)/shard_map/ppermute | solution.py:15
  489.5 8.6 %collective-permute-done.52 = f32[4,128,1]{2,1,0:T(8,128)S(1)} collective-permute-done((f32[4,128,1]{2,1,0:T(8,128)S(1)}, f32[4,128,1]{2,1,0:T(8,128)S(1)}, u32[]{:S(2)}, u32[]{:S(2)}) %collective-permute-start.52) | collective-permute-done | bytes 2080 | tf_op jit(solution)/shard_map/ppermute | solution.py:12
  500.9 8.1 %collective-permute-start.55 = (f32[4,128,1]{2,1,0:T(8,128)S(1)}, f32[4,128,1]{2,1,0:T(8,128)S(1)}, u32[]{:S(2)}, u32[]{:S(2)}) collective-permute-start(f32[4,128,1]{2,1,0:T(8,128)S(1)} %get-tuple-element.110), channel_id=1, source_target_pairs={{1,0},{2,1},{3,2},{4,3},{5,4},{6,5},{7,6},{8,7},{9,8},{10,9},{11,1... | collective-permute-start | bytes 6152 | tf_op jit(solution)/shard_map/ppermute | solution.py:15
  509.0 2.4 collective-permute-done.54
  514.1 8.7 %collective-permute-start.57 = (f32[4,128,1]{2,1,0:T(8,128)S(1)}, f32[4,128,1]{2,1,0:T(8,128)S(1)}, u32[]{:S(2)}, u32[]{:S(2)}) collective-permute-start(f32[4,128,1]{2,1,0:T(8,128)S(1)} %get-tuple-element.107), channel_id=1, source_target_pairs={{1,0},{2,1},{3,2},{4,3},{5,4},{6,5},{7,6},{8,7},{9,8},{10,9},{11,1... | collective-permute-start | bytes 6152 | tf_op jit(solution)/shard_map/ppermute | solution.py:15
  526.7 8.6 %collective-permute-done.56 = f32[4,128,1]{2,1,0:T(8,128)S(1)} collective-permute-done((f32[4,128,1]{2,1,0:T(8,128)S(1)}, f32[4,128,1]{2,1,0:T(8,128)S(1)}, u32[]{:S(2)}, u32[]{:S(2)}) %collective-permute-start.56) | collective-permute-done | bytes 2080 | tf_op jit(solution)/shard_map/ppermute | solution.py:12
  538.0 8.1 %collective-permute-start.59 = (f32[4,128,1]{2,1,0:T(8,128)S(1)}, f32[4,128,1]{2,1,0:T(8,128)S(1)}, u32[]{:S(2)}, u32[]{:S(2)}) collective-permute-start(f32[4,128,1]{2,1,0:T(8,128)S(1)} %get-tuple-element.106), channel_id=1, source_target_pairs={{1,0},{2,1},{3,2},{4,3},{5,4},{6,5},{7,6},{8,7},{9,8},{10,9},{11,1... | collective-permute-start | bytes 6152 | tf_op jit(solution)/shard_map/ppermute | solution.py:15
  (200 shorter events, 132.2 us)
Async XLA Ops:
  0.8 7.1 %collective-permute-start.5 = (f32[128,128]{1,0:T(8,128)S(1)}, f32[128,128]{1,0:T(8,128)S(1)}, u32[]{:S(2)}, u32[]{:S(2)}) collective-permute-start(f32[128,128]{1,0:T(8,128)S(1)} %slice_bitcast_fusion.4), channel_id=1, source_target_pairs={{0,64},{64,128},{128,192},{1,65},{65,129},{129,193},{2,66},{66,130... | collective-permute-start | bytes 196616 | tf_op jit(solution)/shard_map/ppermute | solution.py:23
  8.1 12.6 %collective-permute-start.6 = (f32[4,128,1]{2,1,0:T(8,128)S(1)}, f32[4,128,1]{2,1,0:T(8,128)S(1)}, u32[]{:S(2)}, u32[]{:S(2)}) collective-permute-start(f32[4,128,1]{2,1,0:T(8,128)S(1)} %get-tuple-element.133), channel_id=1, source_target_pairs={{0,1},{1,2},{2,3},{3,4},{4,5},{5,6},{6,7},{7,8},{8,9},{9,10},{10,1... | collective-permute-start | bytes 6152 | tf_op jit(solution)/shard_map/ppermute | solution.py:12
  11.2 10.9 %collective-permute-start.7 = (f32[4,128,1]{2,1,0:T(8,128)S(1)}, f32[4,128,1]{2,1,0:T(8,128)S(1)}, u32[]{:S(2)}, u32[]{:S(2)}) collective-permute-start(f32[4,128,1]{2,1,0:T(8,128)S(1)} %get-tuple-element.134), channel_id=1, source_target_pairs={{1,0},{2,1},{3,2},{4,3},{5,4},{6,5},{7,6},{8,7},{9,8},{10,9},{11,1... | collective-permute-start | bytes 6152 | tf_op jit(solution)/shard_map/ppermute | solution.py:15
  23.0 13.3 %collective-permute-start.8 = (f32[4,128,1]{2,1,0:T(8,128)S(1)}, f32[4,128,1]{2,1,0:T(8,128)S(1)}, u32[]{:S(2)}, u32[]{:S(2)}) collective-permute-start(f32[4,128,1]{2,1,0:T(8,128)S(1)} %get-tuple-element.131), channel_id=1, source_target_pairs={{0,1},{1,2},{2,3},{3,4},{4,5},{5,6},{6,7},{7,8},{8,9},{9,10},{10,1... | collective-permute-start | bytes 6152 | tf_op jit(solution)/shard_map/ppermute | solution.py:12
  25.6 12.0 %collective-permute-start.9 = (f32[4,128,1]{2,1,0:T(8,128)S(1)}, f32[4,128,1]{2,1,0:T(8,128)S(1)}, u32[]{:S(2)}, u32[]{:S(2)}) collective-permute-start(f32[4,128,1]{2,1,0:T(8,128)S(1)} %get-tuple-element.132), channel_id=1, source_target_pairs={{1,0},{2,1},{3,2},{4,3},{5,4},{6,5},{7,6},{8,7},{9,8},{10,9},{11,1... | collective-permute-start | bytes 6152 | tf_op jit(solution)/shard_map/ppermute | solution.py:15
  38.4 12.6 %collective-permute-start.11 = (f32[4,128,1]{2,1,0:T(8,128)S(1)}, f32[4,128,1]{2,1,0:T(8,128)S(1)}, u32[]{:S(2)}, u32[]{:S(2)}) collective-permute-start(f32[4,128,1]{2,1,0:T(8,128)S(1)} %get-tuple-element.129), channel_id=1, source_target_pairs={{1,0},{2,1},{3,2},{4,3},{5,4},{6,5},{7,6},{8,7},{9,8},{10,9},{11,1... | collective-permute-start | bytes 6152 | tf_op jit(solution)/shard_map/ppermute | solution.py:15
  47.2 12.6 %collective-permute-start.10 = (f32[4,128,1]{2,1,0:T(8,128)S(1)}, f32[4,128,1]{2,1,0:T(8,128)S(1)}, u32[]{:S(2)}, u32[]{:S(2)}) collective-permute-start(f32[4,128,1]{2,1,0:T(8,128)S(1)} %get-tuple-element.130), channel_id=1, source_target_pairs={{0,1},{1,2},{2,3},{3,4},{4,5},{5,6},{6,7},{7,8},{8,9},{9,10},{10,1... | collective-permute-start | bytes 6152 | tf_op jit(solution)/shard_map/ppermute | solution.py:12
  60.6 12.6 %collective-permute-start.12 = (f32[4,128,1]{2,1,0:T(8,128)S(1)}, f32[4,128,1]{2,1,0:T(8,128)S(1)}, u32[]{:S(2)}, u32[]{:S(2)}) collective-permute-start(f32[4,128,1]{2,1,0:T(8,128)S(1)} %get-tuple-element.127), channel_id=1, source_target_pairs={{0,1},{1,2},{2,3},{3,4},{4,5},{5,6},{6,7},{7,8},{8,9},{9,10},{10,1... | collective-permute-start | bytes 6152 | tf_op jit(solution)/shard_map/ppermute | solution.py:12
  62.5 12.0 %collective-permute-start.13 = (f32[4,128,1]{2,1,0:T(8,128)S(1)}, f32[4,128,1]{2,1,0:T(8,128)S(1)}, u32[]{:S(2)}, u32[]{:S(2)}) collective-permute-start(f32[4,128,1]{2,1,0:T(8,128)S(1)} %get-tuple-element.128), channel_id=1, source_target_pairs={{1,0},{2,1},{3,2},{4,3},{5,4},{6,5},{7,6},{8,7},{9,8},{10,9},{11,1... | collective-permute-start | bytes 6152 | tf_op jit(solution)/shard_map/ppermute | solution.py:15
  75.7 12.5 %collective-permute-start.15 = (f32[4,128,1]{2,1,0:T(8,128)S(1)}, f32[4,128,1]{2,1,0:T(8,128)S(1)}, u32[]{:S(2)}, u32[]{:S(2)}) collective-permute-start(f32[4,128,1]{2,1,0:T(8,128)S(1)} %get-tuple-element.125), channel_id=1, source_target_pairs={{1,0},{2,1},{3,2},{4,3},{5,4},{6,5},{7,6},{8,7},{9,8},{10,9},{11,1... | collective-permute-start | bytes 6152 | tf_op jit(solution)/shard_map/ppermute | solution.py:15
  84.3 14.0 %collective-permute-start.14 = (f32[4,128,1]{2,1,0:T(8,128)S(1)}, f32[4,128,1]{2,1,0:T(8,128)S(1)}, u32[]{:S(2)}, u32[]{:S(2)}) collective-permute-start(f32[4,128,1]{2,1,0:T(8,128)S(1)} %get-tuple-element.126), channel_id=1, source_target_pairs={{0,1},{1,2},{2,3},{3,4},{4,5},{5,6},{6,7},{7,8},{8,9},{9,10},{10,1... | collective-permute-start | bytes 6152 | tf_op jit(solution)/shard_map/ppermute | solution.py:12
  99.2 12.5 %collective-permute-start.16 = (f32[4,128,1]{2,1,0:T(8,128)S(1)}, f32[4,128,1]{2,1,0:T(8,128)S(1)}, u32[]{:S(2)}, u32[]{:S(2)}) collective-permute-start(f32[4,128,1]{2,1,0:T(8,128)S(1)} %get-tuple-element.123), channel_id=1, source_target_pairs={{0,1},{1,2},{2,3},{3,4},{4,5},{5,6},{6,7},{7,8},{8,9},{9,10},{10,1... | collective-permute-start | bytes 6152 | tf_op jit(solution)/shard_map/ppermute | solution.py:12
  101.1 13.6 %collective-permute-start.17 = (f32[4,128,1]{2,1,0:T(8,128)S(1)}, f32[4,128,1]{2,1,0:T(8,128)S(1)}, u32[]{:S(2)}, u32[]{:S(2)}) collective-permute-start(f32[4,128,1]{2,1,0:T(8,128)S(1)} %get-tuple-element.124), channel_id=1, source_target_pairs={{1,0},{2,1},{3,2},{4,3},{5,4},{6,5},{7,6},{8,7},{9,8},{10,9},{11,1... | collective-permute-start | bytes 6152 | tf_op jit(solution)/shard_map/ppermute | solution.py:15
  115.9 12.5 %collective-permute-start.19 = (f32[4,128,1]{2,1,0:T(8,128)S(1)}, f32[4,128,1]{2,1,0:T(8,128)S(1)}, u32[]{:S(2)}, u32[]{:S(2)}) collective-permute-start(f32[4,128,1]{2,1,0:T(8,128)S(1)} %get-tuple-element.121), channel_id=1, source_target_pairs={{1,0},{2,1},{3,2},{4,3},{5,4},{6,5},{7,6},{8,7},{9,8},{10,9},{11,1... | collective-permute-start | bytes 6152 | tf_op jit(solution)/shard_map/ppermute | solution.py:15
  124.6 12.6 %collective-permute-start.18 = (f32[4,128,1]{2,1,0:T(8,128)S(1)}, f32[4,128,1]{2,1,0:T(8,128)S(1)}, u32[]{:S(2)}, u32[]{:S(2)}) collective-permute-start(f32[4,128,1]{2,1,0:T(8,128)S(1)} %get-tuple-element.122), channel_id=1, source_target_pairs={{0,1},{1,2},{2,3},{3,4},{4,5},{5,6},{6,7},{7,8},{8,9},{9,10},{10,1... | collective-permute-start | bytes 6152 | tf_op jit(solution)/shard_map/ppermute | solution.py:12
  138.0 12.6 %collective-permute-start.20 = (f32[4,128,1]{2,1,0:T(8,128)S(1)}, f32[4,128,1]{2,1,0:T(8,128)S(1)}, u32[]{:S(2)}, u32[]{:S(2)}) collective-permute-start(f32[4,128,1]{2,1,0:T(8,128)S(1)} %get-tuple-element.119), channel_id=1, source_target_pairs={{0,1},{1,2},{2,3},{3,4},{4,5},{5,6},{6,7},{7,8},{8,9},{9,10},{10,1... | collective-permute-start | bytes 6152 | tf_op jit(solution)/shard_map/ppermute | solution.py:12
  140.0 12.1 %collective-permute-start.21 = (f32[4,128,1]{2,1,0:T(8,128)S(1)}, f32[4,128,1]{2,1,0:T(8,128)S(1)}, u32[]{:S(2)}, u32[]{:S(2)}) collective-permute-start(f32[4,128,1]{2,1,0:T(8,128)S(1)} %get-tuple-element.120), channel_id=1, source_target_pairs={{1,0},{2,1},{3,2},{4,3},{5,4},{6,5},{7,6},{8,7},{9,8},{10,9},{11,1... | collective-permute-start | bytes 6152 | tf_op jit(solution)/shard_map/ppermute | solution.py:15
  153.3 10.9 %collective-permute-start.23 = (f32[1,128,1]{2,1,0:T(8,128)S(1)}, f32[1,128,1]{2,1,0:T(8,128)S(1)}, u32[]{:S(2)}, u32[]{:S(2)}) collective-permute-start(f32[1,128,1]{2,1,0:T(8,128)S(1)} %get-tuple-element.117), channel_id=1, source_target_pairs={{1,0},{2,1},{3,2},{4,3},{5,4},{6,5},{7,6},{8,7},{9,8},{10,9},{11,1... | collective-permute-start | bytes 1544 | tf_op jit(solution)/shard_map/ppermute | solution.py:15
  161.9 10.4 %collective-permute-start.22 = (f32[1,128,1]{2,1,0:T(8,128)S(1)}, f32[1,128,1]{2,1,0:T(8,128)S(1)}, u32[]{:S(2)}, u32[]{:S(2)}) collective-permute-start(f32[1,128,1]{2,1,0:T(8,128)S(1)} %get-tuple-element.118), channel_id=1, source_target_pairs={{0,1},{1,2},{2,3},{3,4},{4,5},{5,6},{6,7},{7,8},{8,9},{9,10},{10,1... | collective-permute-start | bytes 1544 | tf_op jit(solution)/shard_map/ppermute | solution.py:12
  172.6 10.4 %collective-permute-start.24 = (f32[1,128,1]{2,1,0:T(8,128)S(1)}, f32[1,128,1]{2,1,0:T(8,128)S(1)}, u32[]{:S(2)}, u32[]{:S(2)}) collective-permute-start(f32[1,128,1]{2,1,0:T(8,128)S(1)} %get-tuple-element.159), channel_id=1, source_target_pairs={{0,1},{1,2},{2,3},{3,4},{4,5},{5,6},{6,7},{7,8},{8,9},{9,10},{10,1... | collective-permute-start | bytes 1544 | tf_op jit(solution)/shard_map/ppermute | solution.py:12
  174.6 10.0 %collective-permute-start.25 = (f32[1,128,1]{2,1,0:T(8,128)S(1)}, f32[1,128,1]{2,1,0:T(8,128)S(1)}, u32[]{:S(2)}, u32[]{:S(2)}) collective-permute-start(f32[1,128,1]{2,1,0:T(8,128)S(1)} %get-tuple-element.160), channel_id=1, source_target_pairs={{1,0},{2,1},{3,2},{4,3},{5,4},{6,5},{7,6},{8,7},{9,8},{10,9},{11,1... | collective-permute-start | bytes 1544 | tf_op jit(solution)/shard_map/ppermute | solution.py:15
  185.0 10.4 %collective-permute-start.27 = (f32[1,128,1]{2,1,0:T(8,128)S(1)}, f32[1,128,1]{2,1,0:T(8,128)S(1)}, u32[]{:S(2)}, u32[]{:S(2)}) collective-permute-start(f32[1,128,1]{2,1,0:T(8,128)S(1)} %get-tuple-element.157), channel_id=1, source_target_pairs={{1,0},{2,1},{3,2},{4,3},{5,4},{6,5},{7,6},{8,7},{9,8},{10,9},{11,1... | collective-permute-start | bytes 1544 | tf_op jit(solution)/shard_map/ppermute | solution.py:15
  193.5 10.4 %collective-permute-start.26 = (f32[1,128,1]{2,1,0:T(8,128)S(1)}, f32[1,128,1]{2,1,0:T(8,128)S(1)}, u32[]{:S(2)}, u32[]{:S(2)}) collective-permute-start(f32[1,128,1]{2,1,0:T(8,128)S(1)} %get-tuple-element.158), channel_id=1, source_target_pairs={{0,1},{1,2},{2,3},{3,4},{4,5},{5,6},{6,7},{7,8},{8,9},{9,10},{10,1... | collective-permute-start | bytes 1544 | tf_op jit(solution)/shard_map/ppermute | solution.py:12
  204.3 10.4 %collective-permute-start.28 = (f32[1,128,1]{2,1,0:T(8,128)S(1)}, f32[1,128,1]{2,1,0:T(8,128)S(1)}, u32[]{:S(2)}, u32[]{:S(2)}) collective-permute-start(f32[1,128,1]{2,1,0:T(8,128)S(1)} %get-tuple-element.155), channel_id=1, source_target_pairs={{0,1},{1,2},{2,3},{3,4},{4,5},{5,6},{6,7},{7,8},{8,9},{9,10},{10,1... | collective-permute-start | bytes 1544 | tf_op jit(solution)/shard_map/ppermute | solution.py:12
  206.2 10.0 %collective-permute-start.29 = (f32[1,128,1]{2,1,0:T(8,128)S(1)}, f32[1,128,1]{2,1,0:T(8,128)S(1)}, u32[]{:S(2)}, u32[]{:S(2)}) collective-permute-start(f32[1,128,1]{2,1,0:T(8,128)S(1)} %get-tuple-element.156), channel_id=1, source_target_pairs={{1,0},{2,1},{3,2},{4,3},{5,4},{6,5},{7,6},{8,7},{9,8},{10,9},{11,1... | collective-permute-start | bytes 1544 | tf_op jit(solution)/shard_map/ppermute | solution.py:15
  216.7 10.4 %collective-permute-start.31 = (f32[1,128,1]{2,1,0:T(8,128)S(1)}, f32[1,128,1]{2,1,0:T(8,128)S(1)}, u32[]{:S(2)}, u32[]{:S(2)}) collective-permute-start(f32[1,128,1]{2,1,0:T(8,128)S(1)} %get-tuple-element.153), channel_id=1, source_target_pairs={{1,0},{2,1},{3,2},{4,3},{5,4},{6,5},{7,6},{8,7},{9,8},{10,9},{11,1... | collective-permute-start | bytes 1544 | tf_op jit(solution)/shard_map/ppermute | solution.py:15
  225.2 10.4 %collective-permute-start.30 = (f32[1,128,1]{2,1,0:T(8,128)S(1)}, f32[1,128,1]{2,1,0:T(8,128)S(1)}, u32[]{:S(2)}, u32[]{:S(2)}) collective-permute-start(f32[1,128,1]{2,1,0:T(8,128)S(1)} %get-tuple-element.154), channel_id=1, source_target_pairs={{0,1},{1,2},{2,3},{3,4},{4,5},{5,6},{6,7},{7,8},{8,9},{9,10},{10,1... | collective-permute-start | bytes 1544 | tf_op jit(solution)/shard_map/ppermute | solution.py:12
  236.0 10.4 %collective-permute-start.32 = (f32[1,128,1]{2,1,0:T(8,128)S(1)}, f32[1,128,1]{2,1,0:T(8,128)S(1)}, u32[]{:S(2)}, u32[]{:S(2)}) collective-permute-start(f32[1,128,1]{2,1,0:T(8,128)S(1)} %get-tuple-element.151), channel_id=1, source_target_pairs={{0,1},{1,2},{2,3},{3,4},{4,5},{5,6},{6,7},{7,8},{8,9},{9,10},{10,1... | collective-permute-start | bytes 1544 | tf_op jit(solution)/shard_map/ppermute | solution.py:12
  237.9 10.0 %collective-permute-start.33 = (f32[1,128,1]{2,1,0:T(8,128)S(1)}, f32[1,128,1]{2,1,0:T(8,128)S(1)}, u32[]{:S(2)}, u32[]{:S(2)}) collective-permute-start(f32[1,128,1]{2,1,0:T(8,128)S(1)} %get-tuple-element.152), channel_id=1, source_target_pairs={{1,0},{2,1},{3,2},{4,3},{5,4},{6,5},{7,6},{8,7},{9,8},{10,9},{11,1... | collective-permute-start | bytes 1544 | tf_op jit(solution)/shard_map/ppermute | solution.py:15
  248.4 10.4 %collective-permute-start = (f32[1,128,1]{2,1,0:T(8,128)S(1)}, f32[1,128,1]{2,1,0:T(8,128)S(1)}, u32[]{:S(2)}, u32[]{:S(2)}) collective-permute-start(f32[1,128,1]{2,1,0:T(8,128)S(1)} %get-tuple-element.208), channel_id=1, source_target_pairs={{1,0},{2,1},{3,2},{4,3},{5,4},{6,5},{7,6},{8,7},{9,8},{10,9},{11,1... | collective-permute-start | bytes 1544 | tf_op jit(solution)/shard_map/while/body/eval_jaxpr/ppermute | solution.py:15
  256.9 10.4 %collective-permute-start.1 = (f32[1,128,1]{2,1,0:T(8,128)S(1)}, f32[1,128,1]{2,1,0:T(8,128)S(1)}, u32[]{:S(2)}, u32[]{:S(2)}) collective-permute-start(f32[1,128,1]{2,1,0:T(8,128)S(1)} %get-tuple-element.209), channel_id=1, source_target_pairs={{0,1},{1,2},{2,3},{3,4},{4,5},{5,6},{6,7},{7,8},{8,9},{9,10},{10,1... | collective-permute-start | bytes 1544 | tf_op jit(solution)/shard_map/while/body/eval_jaxpr/ppermute | solution.py:12
  269.6 10.4 %collective-permute-start.3 = (f32[1,128,1]{2,1,0:T(8,128)S(1)}, f32[1,128,1]{2,1,0:T(8,128)S(1)}, u32[]{:S(2)}, u32[]{:S(2)}) collective-permute-start(f32[1,128,1]{2,1,0:T(8,128)S(1)} %get-tuple-element.211), channel_id=1, source_target_pairs={{0,1},{1,2},{2,3},{3,4},{4,5},{5,6},{6,7},{7,8},{8,9},{9,10},{10,1... | collective-permute-start | bytes 1544 | tf_op jit(solution)/shard_map/while/body/eval_jaxpr/ppermute | solution.py:12
  280.3 7.1 %collective-permute-start.4 = (f32[128,128]{1,0:T(8,128)S(1)}, f32[128,128]{1,0:T(8,128)S(1)}, u32[]{:S(2)}, u32[]{:S(2)}) collective-permute-start(f32[128,128]{1,0:T(8,128)S(1)} %bitcast_add_fusion.2), channel_id=1, source_target_pairs={{0,64},{64,128},{128,192},{1,65},{65,129},{129,193},{2,66},{66,130... | collective-permute-start | bytes 196616 | tf_op jit(solution)/shard_map/while/body/eval_jaxpr/ppermute | solution.py:23
  289.5 10.4 %collective-permute-start.1 = (f32[1,128,1]{2,1,0:T(8,128)S(1)}, f32[1,128,1]{2,1,0:T(8,128)S(1)}, u32[]{:S(2)}, u32[]{:S(2)}) collective-permute-start(f32[1,128,1]{2,1,0:T(8,128)S(1)} %get-tuple-element.209), channel_id=1, source_target_pairs={{0,1},{1,2},{2,3},{3,4},{4,5},{5,6},{6,7},{7,8},{8,9},{9,10},{10,1... | collective-permute-start | bytes 1544 | tf_op jit(solution)/shard_map/while/body/eval_jaxpr/ppermute | solution.py:12
  302.2 10.4 %collective-permute-start.3 = (f32[1,128,1]{2,1,0:T(8,128)S(1)}, f32[1,128,1]{2,1,0:T(8,128)S(1)}, u32[]{:S(2)}, u32[]{:S(2)}) collective-permute-start(f32[1,128,1]{2,1,0:T(8,128)S(1)} %get-tuple-element.211), channel_id=1, source_target_pairs={{0,1},{1,2},{2,3},{3,4},{4,5},{5,6},{6,7},{7,8},{8,9},{9,10},{10,1... | collective-permute-start | bytes 1544 | tf_op jit(solution)/shard_map/while/body/eval_jaxpr/ppermute | solution.py:12
  312.9 7.1 %collective-permute-start.4 = (f32[128,128]{1,0:T(8,128)S(1)}, f32[128,128]{1,0:T(8,128)S(1)}, u32[]{:S(2)}, u32[]{:S(2)}) collective-permute-start(f32[128,128]{1,0:T(8,128)S(1)} %bitcast_add_fusion.2), channel_id=1, source_target_pairs={{0,64},{64,128},{128,192},{1,65},{65,129},{129,193},{2,66},{66,130... | collective-permute-start | bytes 196616 | tf_op jit(solution)/shard_map/while/body/eval_jaxpr/ppermute | solution.py:23
  322.0 10.4 %collective-permute-start.1 = (f32[1,128,1]{2,1,0:T(8,128)S(1)}, f32[1,128,1]{2,1,0:T(8,128)S(1)}, u32[]{:S(2)}, u32[]{:S(2)}) collective-permute-start(f32[1,128,1]{2,1,0:T(8,128)S(1)} %get-tuple-element.209), channel_id=1, source_target_pairs={{0,1},{1,2},{2,3},{3,4},{4,5},{5,6},{6,7},{7,8},{8,9},{9,10},{10,1... | collective-permute-start | bytes 1544 | tf_op jit(solution)/shard_map/while/body/eval_jaxpr/ppermute | solution.py:12
  334.7 10.4 %collective-permute-start.3 = (f32[1,128,1]{2,1,0:T(8,128)S(1)}, f32[1,128,1]{2,1,0:T(8,128)S(1)}, u32[]{:S(2)}, u32[]{:S(2)}) collective-permute-start(f32[1,128,1]{2,1,0:T(8,128)S(1)} %get-tuple-element.211), channel_id=1, source_target_pairs={{0,1},{1,2},{2,3},{3,4},{4,5},{5,6},{6,7},{7,8},{8,9},{9,10},{10,1... | collective-permute-start | bytes 1544 | tf_op jit(solution)/shard_map/while/body/eval_jaxpr/ppermute | solution.py:12
  345.5 7.1 %collective-permute-start.4 = (f32[128,128]{1,0:T(8,128)S(1)}, f32[128,128]{1,0:T(8,128)S(1)}, u32[]{:S(2)}, u32[]{:S(2)}) collective-permute-start(f32[128,128]{1,0:T(8,128)S(1)} %bitcast_add_fusion.2), channel_id=1, source_target_pairs={{0,64},{64,128},{128,192},{1,65},{65,129},{129,193},{2,66},{66,130... | collective-permute-start | bytes 196616 | tf_op jit(solution)/shard_map/while/body/eval_jaxpr/ppermute | solution.py:23
  352.7 10.4 %collective-permute-start.34 = (f32[1,128,1]{2,1,0:T(8,128)S(1)}, f32[1,128,1]{2,1,0:T(8,128)S(1)}, u32[]{:S(2)}, u32[]{:S(2)}) collective-permute-start(f32[1,128,1]{2,1,0:T(8,128)S(1)} %get-tuple-element.149), channel_id=1, source_target_pairs={{0,1},{1,2},{2,3},{3,4},{4,5},{5,6},{6,7},{7,8},{8,9},{9,10},{10,1... | collective-permute-start | bytes 1544 | tf_op jit(solution)/shard_map/ppermute | solution.py:12
  354.6 10.0 %collective-permute-start.35 = (f32[1,128,1]{2,1,0:T(8,128)S(1)}, f32[1,128,1]{2,1,0:T(8,128)S(1)}, u32[]{:S(2)}, u32[]{:S(2)}) collective-permute-start(f32[1,128,1]{2,1,0:T(8,128)S(1)} %get-tuple-element.150), channel_id=1, source_target_pairs={{1,0},{2,1},{3,2},{4,3},{5,4},{6,5},{7,6},{8,7},{9,8},{10,9},{11,1... | collective-permute-start | bytes 1544 | tf_op jit(solution)/shard_map/ppermute | solution.py:15
  365.0 10.8 %collective-permute-start.36 = (f32[1,128,1]{2,1,0:T(8,128)S(1)}, f32[1,128,1]{2,1,0:T(8,128)S(1)}, u32[]{:S(2)}, u32[]{:S(2)}) collective-permute-start(f32[1,128,1]{2,1,0:T(8,128)S(1)} %get-tuple-element.145), channel_id=1, source_target_pairs={{0,1},{1,2},{2,3},{3,4},{4,5},{5,6},{6,7},{7,8},{8,9},{9,10},{10,1... | collective-permute-start | bytes 1544 | tf_op jit(solution)/shard_map/ppermute | solution.py:12
  366.9 10.4 %collective-permute-start.37 = (f32[1,128,1]{2,1,0:T(8,128)S(1)}, f32[1,128,1]{2,1,0:T(8,128)S(1)}, u32[]{:S(2)}, u32[]{:S(2)}) collective-permute-start(f32[1,128,1]{2,1,0:T(8,128)S(1)} %get-tuple-element.146), channel_id=1, source_target_pairs={{1,0},{2,1},{3,2},{4,3},{5,4},{6,5},{7,6},{8,7},{9,8},{10,9},{11,1... | collective-permute-start | bytes 1544 | tf_op jit(solution)/shard_map/ppermute | solution.py:15
  377.8 10.4 %collective-permute-start.39 = (f32[1,128,1]{2,1,0:T(8,128)S(1)}, f32[1,128,1]{2,1,0:T(8,128)S(1)}, u32[]{:S(2)}, u32[]{:S(2)}) collective-permute-start(f32[1,128,1]{2,1,0:T(8,128)S(1)} %get-tuple-element.143), channel_id=1, source_target_pairs={{1,0},{2,1},{3,2},{4,3},{5,4},{6,5},{7,6},{8,7},{9,8},{10,9},{11,1... | collective-permute-start | bytes 1544 | tf_op jit(solution)/shard_map/ppermute | solution.py:15
  386.3 10.4 %collective-permute-start.38 = (f32[1,128,1]{2,1,0:T(8,128)S(1)}, f32[1,128,1]{2,1,0:T(8,128)S(1)}, u32[]{:S(2)}, u32[]{:S(2)}) collective-permute-start(f32[1,128,1]{2,1,0:T(8,128)S(1)} %get-tuple-element.144), channel_id=1, source_target_pairs={{0,1},{1,2},{2,3},{3,4},{4,5},{5,6},{6,7},{7,8},{8,9},{9,10},{10,1... | collective-permute-start | bytes 1544 | tf_op jit(solution)/shard_map/ppermute | solution.py:12
  397.0 20.2 %collective-permute-start.40 = (f32[1,128,1]{2,1,0:T(8,128)S(1)}, f32[1,128,1]{2,1,0:T(8,128)S(1)}, u32[]{:S(2)}, u32[]{:S(2)}) collective-permute-start(f32[1,128,1]{2,1,0:T(8,128)S(1)} %get-tuple-element.141), channel_id=1, source_target_pairs={{0,1},{1,2},{2,3},{3,4},{4,5},{5,6},{6,7},{7,8},{8,9},{9,10},{10,1... | collective-permute-start | bytes 1544 | tf_op jit(solution)/shard_map/ppermute | solution.py:12
  398.9 18.3 %collective-permute-start.41 = (f32[1,128,1]{2,1,0:T(8,128)S(1)}, f32[1,128,1]{2,1,0:T(8,128)S(1)}, u32[]{:S(2)}, u32[]{:S(2)}) collective-permute-start(f32[1,128,1]{2,1,0:T(8,128)S(1)} %get-tuple-element.142), channel_id=1, source_target_pairs={{1,0},{2,1},{3,2},{4,3},{5,4},{6,5},{7,6},{8,7},{9,8},{10,9},{11,1... | collective-permute-start | bytes 1544 | tf_op jit(solution)/shard_map/ppermute | solution.py:15
  407.2 16.4 %collective-permute-start.46 = (f32[1,128,1]{2,1,0:T(8,128)S(1)}, f32[1,128,1]{2,1,0:T(8,128)S(1)}, u32[]{:S(2)}, u32[]{:S(2)}) collective-permute-start(f32[1,128,1]{2,1,0:T(8,128)S(1)} %get-tuple-element.147), channel_id=1, source_target_pairs={{0,1},{1,2},{2,3},{3,4},{4,5},{5,6},{6,7},{7,8},{8,9},{9,10},{10,1... | collective-permute-start | bytes 1544 | tf_op jit(solution)/shard_map/ppermute | solution.py:12
  409.1 14.5 %collective-permute-start.47 = (f32[1,128,1]{2,1,0:T(8,128)S(1)}, f32[1,128,1]{2,1,0:T(8,128)S(1)}, u32[]{:S(2)}, u32[]{:S(2)}) collective-permute-start(f32[1,128,1]{2,1,0:T(8,128)S(1)} %get-tuple-element.148), channel_id=1, source_target_pairs={{1,0},{2,1},{3,2},{4,3},{5,4},{6,5},{7,6},{8,7},{9,8},{10,9},{11,1... | collective-permute-start | bytes 1544 | tf_op jit(solution)/shard_map/ppermute | solution.py:15
  419.6 10.7 %collective-permute-start.42 = (f32[1,128,1]{2,1,0:T(8,128)S(1)}, f32[1,128,1]{2,1,0:T(8,128)S(1)}, u32[]{:S(2)}, u32[]{:S(2)}) collective-permute-start(f32[1,128,1]{2,1,0:T(8,128)S(1)} %get-tuple-element.140), channel_id=1, source_target_pairs={{0,1},{1,2},{2,3},{3,4},{4,5},{5,6},{6,7},{7,8},{8,9},{9,10},{10,1... | collective-permute-start | bytes 1544 | tf_op jit(solution)/shard_map/ppermute | solution.py:12
  430.7 10.8 %collective-permute-start.44 = (f32[1,128,1]{2,1,0:T(8,128)S(1)}, f32[1,128,1]{2,1,0:T(8,128)S(1)}, u32[]{:S(2)}, u32[]{:S(2)}) collective-permute-start(f32[1,128,1]{2,1,0:T(8,128)S(1)} %get-tuple-element.137), channel_id=1, source_target_pairs={{0,1},{1,2},{2,3},{3,4},{4,5},{5,6},{6,7},{7,8},{8,9},{9,10},{10,1... | collective-permute-start | bytes 1544 | tf_op jit(solution)/shard_map/ppermute | solution.py:12
  432.6 10.5 %collective-permute-start.45 = (f32[1,128,1]{2,1,0:T(8,128)S(1)}, f32[1,128,1]{2,1,0:T(8,128)S(1)}, u32[]{:S(2)}, u32[]{:S(2)}) collective-permute-start(f32[1,128,1]{2,1,0:T(8,128)S(1)} %get-tuple-element.138), channel_id=1, source_target_pairs={{1,0},{2,1},{3,2},{4,3},{5,4},{6,5},{7,6},{8,7},{9,8},{10,9},{11,1... | collective-permute-start | bytes 1544 | tf_op jit(solution)/shard_map/ppermute | solution.py:15
  443.7 14.2 %collective-permute-start.48 = (f32[4,128,1]{2,1,0:T(8,128)S(1)}, f32[4,128,1]{2,1,0:T(8,128)S(1)}, u32[]{:S(2)}, u32[]{:S(2)}) collective-permute-start(f32[4,128,1]{2,1,0:T(8,128)S(1)} %get-tuple-element.115), channel_id=1, source_target_pairs={{0,1},{1,2},{2,3},{3,4},{4,5},{5,6},{6,7},{7,8},{8,9},{9,10},{10,1... | collective-permute-start | bytes 6152 | tf_op jit(solution)/shard_map/ppermute | solution.py:12
  445.6 14.0 %collective-permute-start.49 = (f32[4,128,1]{2,1,0:T(8,128)S(1)}, f32[4,128,1]{2,1,0:T(8,128)S(1)}, u32[]{:S(2)}, u32[]{:S(2)}) collective-permute-start(f32[4,128,1]{2,1,0:T(8,128)S(1)} %get-tuple-element.116), channel_id=1, source_target_pairs={{1,0},{2,1},{3,2},{4,3},{5,4},{6,5},{7,6},{8,7},{9,8},{10,9},{11,1... | collective-permute-start | bytes 6152 | tf_op jit(solution)/shard_map/ppermute | solution.py:15
  460.5 13.0 %collective-permute-start.50 = (f32[4,128,1]{2,1,0:T(8,128)S(1)}, f32[4,128,1]{2,1,0:T(8,128)S(1)}, u32[]{:S(2)}, u32[]{:S(2)}) collective-permute-start(f32[4,128,1]{2,1,0:T(8,128)S(1)} %get-tuple-element.113), channel_id=1, source_target_pairs={{0,1},{1,2},{2,3},{3,4},{4,5},{5,6},{6,7},{7,8},{8,9},{9,10},{10,1... | collective-permute-start | bytes 6152 | tf_op jit(solution)/shard_map/ppermute | solution.py:12
  462.6 13.4 %collective-permute-start.51 = (f32[4,128,1]{2,1,0:T(8,128)S(1)}, f32[4,128,1]{2,1,0:T(8,128)S(1)}, u32[]{:S(2)}, u32[]{:S(2)}) collective-permute-start(f32[4,128,1]{2,1,0:T(8,128)S(1)} %get-tuple-element.114), channel_id=1, source_target_pairs={{1,0},{2,1},{3,2},{4,3},{5,4},{6,5},{7,6},{8,7},{9,8},{10,9},{11,1... | collective-permute-start | bytes 6152 | tf_op jit(solution)/shard_map/ppermute | solution.py:15
  476.9 12.5 %collective-permute-start.53 = (f32[4,128,1]{2,1,0:T(8,128)S(1)}, f32[4,128,1]{2,1,0:T(8,128)S(1)}, u32[]{:S(2)}, u32[]{:S(2)}) collective-permute-start(f32[4,128,1]{2,1,0:T(8,128)S(1)} %get-tuple-element.111), channel_id=1, source_target_pairs={{1,0},{2,1},{3,2},{4,3},{5,4},{6,5},{7,6},{8,7},{9,8},{10,9},{11,1... | collective-permute-start | bytes 6152 | tf_op jit(solution)/shard_map/ppermute | solution.py:15
  485.6 12.5 %collective-permute-start.52 = (f32[4,128,1]{2,1,0:T(8,128)S(1)}, f32[4,128,1]{2,1,0:T(8,128)S(1)}, u32[]{:S(2)}, u32[]{:S(2)}) collective-permute-start(f32[4,128,1]{2,1,0:T(8,128)S(1)} %get-tuple-element.112), channel_id=1, source_target_pairs={{0,1},{1,2},{2,3},{3,4},{4,5},{5,6},{6,7},{7,8},{8,9},{9,10},{10,1... | collective-permute-start | bytes 6152 | tf_op jit(solution)/shard_map/ppermute | solution.py:12
  498.9 12.5 %collective-permute-start.54 = (f32[4,128,1]{2,1,0:T(8,128)S(1)}, f32[4,128,1]{2,1,0:T(8,128)S(1)}, u32[]{:S(2)}, u32[]{:S(2)}) collective-permute-start(f32[4,128,1]{2,1,0:T(8,128)S(1)} %get-tuple-element.109), channel_id=1, source_target_pairs={{0,1},{1,2},{2,3},{3,4},{4,5},{5,6},{6,7},{7,8},{8,9},{9,10},{10,1... | collective-permute-start | bytes 6152 | tf_op jit(solution)/shard_map/ppermute | solution.py:12
  500.9 12.1 %collective-permute-start.55 = (f32[4,128,1]{2,1,0:T(8,128)S(1)}, f32[4,128,1]{2,1,0:T(8,128)S(1)}, u32[]{:S(2)}, u32[]{:S(2)}) collective-permute-start(f32[4,128,1]{2,1,0:T(8,128)S(1)} %get-tuple-element.110), channel_id=1, source_target_pairs={{1,0},{2,1},{3,2},{4,3},{5,4},{6,5},{7,6},{8,7},{9,8},{10,9},{11,1... | collective-permute-start | bytes 6152 | tf_op jit(solution)/shard_map/ppermute | solution.py:15
  514.1 12.5 %collective-permute-start.57 = (f32[4,128,1]{2,1,0:T(8,128)S(1)}, f32[4,128,1]{2,1,0:T(8,128)S(1)}, u32[]{:S(2)}, u32[]{:S(2)}) collective-permute-start(f32[4,128,1]{2,1,0:T(8,128)S(1)} %get-tuple-element.107), channel_id=1, source_target_pairs={{1,0},{2,1},{3,2},{4,3},{5,4},{6,5},{7,6},{8,7},{9,8},{10,9},{11,1... | collective-permute-start | bytes 6152 | tf_op jit(solution)/shard_map/ppermute | solution.py:15
  522.8 12.5 %collective-permute-start.56 = (f32[4,128,1]{2,1,0:T(8,128)S(1)}, f32[4,128,1]{2,1,0:T(8,128)S(1)}, u32[]{:S(2)}, u32[]{:S(2)}) collective-permute-start(f32[4,128,1]{2,1,0:T(8,128)S(1)} %get-tuple-element.108), channel_id=1, source_target_pairs={{0,1},{1,2},{2,3},{3,4},{4,5},{5,6},{6,7},{7,8},{8,9},{9,10},{10,1... | collective-permute-start | bytes 6152 | tf_op jit(solution)/shard_map/ppermute | solution.py:12
  536.1 12.5 %collective-permute-start.58 = (f32[4,128,1]{2,1,0:T(8,128)S(1)}, f32[4,128,1]{2,1,0:T(8,128)S(1)}, u32[]{:S(2)}, u32[]{:S(2)}) collective-permute-start(f32[4,128,1]{2,1,0:T(8,128)S(1)} %get-tuple-element.105), channel_id=1, source_target_pairs={{0,1},{1,2},{2,3},{3,4},{4,5},{5,6},{6,7},{7,8},{8,9},{9,10},{10,1... | collective-permute-start | bytes 6152 | tf_op jit(solution)/shard_map/ppermute | solution.py:12
  538.0 12.0 %collective-permute-start.59 = (f32[4,128,1]{2,1,0:T(8,128)S(1)}, f32[4,128,1]{2,1,0:T(8,128)S(1)}, u32[]{:S(2)}, u32[]{:S(2)}) collective-permute-start(f32[4,128,1]{2,1,0:T(8,128)S(1)} %get-tuple-element.106), channel_id=1, source_target_pairs={{1,0},{2,1},{3,2},{4,3},{5,4},{6,5},{7,6},{8,7},{9,8},{10,9},{11,1... | collective-permute-start | bytes 6152 | tf_op jit(solution)/shard_map/ppermute | solution.py:15
  (12 other events, 94.2 us)
where the time goes:
time: 558 us; the launch traced here: 552 us
  starting transfers between devices  321 us (58%)
  waiting for transfers between devices  206 us (37%)
  other arithmetic  18.1 us (3%)
  local copies, waits for them, and re-layouts  6 us (1%)
    ppermute x33, starting transfers between devices, extended(): lax.ppermute(lax.slice_in_dim(block, 0, width, axis=dim), axis, backward)  236 us
    ppermute x33, waiting for transfers between devices, extended(): lax.ppermute(lax.slice_in_dim(block, block.shape[dim] - width, None, axis...  149 us
    ppermute x33, starting transfers between devices, extended(): lax.ppermute(lax.slice_in_dim(block, block.shape[dim] - width, None, axis...  77.4 us
    ppermute x33, waiting for transfers between devices, extended(): lax.ppermute(lax.slice_in_dim(block, 0, width, axis=dim), axis, backward)  37.3 us
    ppermute x4, waiting for transfers between devices, from_behind(): return lax.ppermute(x, axis, pairs)  19.6 us
  transfers between devices with their start and end apart: 70, of which 62 were waited for; matrix products, arithmetic and copies ran while one was open for 0% of the time, Pallas kernels for 0%

commit v1 on v0

v1 whole, which is shorter than its diff:
```python
import functools

import jax
import jax.numpy as jnp
from jax import lax
from jax.experimental import pallas as pl
from jax.experimental.pallas import tpu as pltpu
from jax.sharding import PartitionSpec as P

MESH = pl.DeviceIdType.MESH
C = 128
H = 16
W = C + 2 * H
Z = 8
N = W + 2 * Z
F32 = jnp.float32


def stencil(k, v, south, north):
    west = pltpu.roll(v, 1, 1)
    east = pltpu.roll(v, v.shape[1] - 1, 1)
    return (k[0] * v + k[1] * west) + (k[2] * east + (k[3] * south + k[4] * north))


def around(ref, at, lo, n):
    return ref[at + (pl.ds(lo, n),)], ref[at + (pl.ds(lo - 1, n),)], ref[at + (pl.ds(lo + 1, n),)]


def propagate(coef, m, src, mid, count, width, emit):
    n = C + 2 * width
    lo = Z + H - width
    k = [coef[m, j, pl.ds(H - width, n), :] for j in range(5)]
    where = [(i,) for i in range(count)] if count else [()]
    for at in where:
        v, south, north = around(src, at, lo, n)
        mid[at + (pl.ds(lo, n),)] = stencil(k, v, south, north)
    for at in where:
        v, south, north = around(mid, at, lo, n)
        emit(at, 0.5 * (src[at + (pl.ds(lo, n),)] + stencil(k, v, south, north)))


def kernel(u_hbm, guess_hbm, forcing_hbm, sx_hbm, sy_hbm, d_hbm, out,
           raw_k, raw_u, raw_g, raw_f, prev, kraw, coef, hold, g3, f2, f3, sa, sb, sc, rp, rf,
           la, lb, lc, y1p, y1, y2, y1f, y2f, e1p, e1, bf, rl, rr, yl, yr, rsl, rsr,
           lsem, ssem, rsem):
    tm, sx, c = lax.axis_index("tm"), lax.axis_index("sx"), lax.axis_index("sy")
    count = lax.axis_size("sy")
    place = 2 * tm + sx
    right, left = lax.rem(c + 1, count), lax.rem(c + count - 1, count)
    has_left = jnp.where(c > 0, 1.0, 0.0).astype(F32)
    has_right = jnp.where(c < count - 1, 1.0, 0.0).astype(F32)

    def fetch(src, dst, i):
        copy = pltpu.make_async_copy(src, dst, lsem.at[i])
        copy.start()
        return copy

    loads_k = [fetch(ref, raw_k.at[i], i) for i, ref in enumerate((sx_hbm, sy_hbm, d_hbm))]
    load_g = fetch(guess_hbm, raw_g, 3)
    load_u = fetch(u_hbm, raw_u, 4)
    load_f = fetch(forcing_hbm, raw_f, 5)

    barrier = pltpu.get_barrier_semaphore()

    def greet(*device):
        pl.semaphore_signal(barrier, inc=1, device_id=device, device_id_type=MESH)

    greet(tm, sx, left)
    greet(tm, sx, right)
    greet(tm, 1 - sx, c)

    @pl.when(place == 1)
    def _():
        greet(1, 0, c)
        greet(1, 1, c)

    @pl.when(tm == 1)
    def _():
        greet(0, 1, c)

    for ref in (sa, sb, sc, rp, rf, la, lb, lc, bf):
        ref[...] = jnp.zeros_like(ref)
    for ref in (y1p, y1f, y2f, y2, e1p, e1):
        ref[pl.ds(0, Z), :] = jnp.zeros((Z, ref.shape[1]), F32)
        ref[pl.ds(N - Z, Z), :] = jnp.zeros((Z, ref.shape[1]), F32)

    for i, load in enumerate(loads_k):
        load.wait()
        kraw[i, pl.ds(H, C), :] = raw_k[i].T

    pl.semaphore_wait(barrier, jnp.where(place == 1, 5, 3 + tm))

    sent = []

    def send(i, src, dst, device):
        copy = pltpu.make_async_remote_copy(src_ref=src, dst_ref=dst, send_sem=ssem.at[i], recv_sem=rsem.at[i],
                                            device_id=device, device_id_type=MESH)
        copy.start()
        return copy

    def both(i, to_right, at_right, to_left, at_left):
        pair = (send(i, to_right, at_right, (tm, sx, right)), send(i + 1, to_left, at_left, (tm, sx, left)))
        sent.extend(pair)
        return pair

    def arrive(*copies):
        for copy in copies:
            copy.wait_recv()

    halo_k = both(0, kraw.at[:, pl.ds(C, H), :], kraw.at[:, pl.ds(0, H), :],
                  kraw.at[:, pl.ds(H, H), :], kraw.at[:, pl.ds(H + C, H), :])

    load_g.wait()
    after = place + 1
    onward = (lax.div(after, 2), lax.rem(after, 2), c)
    prev_copy = pltpu.make_async_remote_copy(src_ref=raw_g.at[3], dst_ref=prev, send_sem=ssem.at[2], recv_sem=rsem.at[2],
                                             device_id=onward, device_id_type=MESH)

    @pl.when(place < 3)
    def _():
        prev_copy.start()

    for i in range(3):
        hold[1 + i, pl.ds(8, C), :] = raw_g[i].T
    g3[...] = raw_g[3].T
    load_u.wait()
    load_f.wait()
    for j in range(4):
        hold[4 + j, pl.ds(8, C), :] = raw_f[4 * j].T
        hold[8 + j, pl.ds(8, C), :] = raw_f[4 * j + 1].T
    halo_h = both(3, hold.at[pl.ds(1, 11), pl.ds(C, 8), :], hold.at[pl.ds(1, 11), pl.ds(0, 8), :],
                  hold.at[pl.ds(1, 11), pl.ds(8, 8), :], hold.at[pl.ds(1, 11), pl.ds(8 + C, 8), :])
    for j in range(4):
        f2[j] = raw_f[4 * j + 2].T
        f3[j] = raw_f[4 * j + 3].T

    @pl.when(place == 0)
    def _():
        hold[0, pl.ds(8, C), :] = raw_u[...].T

    @pl.when(place > 0)
    def _():
        prev_copy.wait_recv()
        hold[0, pl.ds(8, C), :] = prev[...].T

    halo_s = both(5, hold.at[0, pl.ds(C, 8), :], hold.at[0, pl.ds(0, 8), :],
                  hold.at[0, pl.ds(8, 8), :], hold.at[0, pl.ds(8 + C, 8), :])

    arrive(*halo_k)
    row = lax.broadcasted_iota(jnp.int32, (W, C), 1)
    column = lax.broadcasted_iota(jnp.int32, (W, C), 0)
    inside = jnp.where(column < H, has_left, jnp.where(column >= H + C, has_right, 1.0))
    speed_x, speed_y, diffusion = kraw[0] * inside, kraw[1] * inside, kraw[2] * inside
    west = jnp.maximum(speed_x, 0.0) + diffusion
    east = diffusion - jnp.minimum(speed_x, 0.0)
    south = jnp.maximum(speed_y, 0.0) + diffusion
    north = diffusion - jnp.minimum(speed_y, 0.0)
    centre = (west + east) + (south + north)
    west = jnp.where(row == 0, 0.0, west)
    east = jnp.where(row == C - 1, 0.0, east)
    for m, factor in enumerate((1.0, 4.0, 16.0)):
        coef[m, 0] = 1.0 - factor * centre
        coef[m, 1] = factor * west
        coef[m, 2] = factor * east
        coef[m, 3] = factor * south
        coef[m, 4] = factor * north

    main = pl.ds(Z + H, C)

    for i in range(4):
        sa[i, main, :] = hold[i, pl.ds(8, C), :]

    def into(dst, source):
        def emit(at, x):
            dst[at + (pl.ds(Z + H - 8, 8),)] = x[:8]
            dst[at + (main,)] = x[8 : 8 + C] + source(at[0])
            dst[at + (pl.ds(Z + H + C, 8),)] = x[8 + C :]
        return emit

    propagate(coef, 0, sa, sb, 4, 8, into(sc, lambda i: hold[4 + i, pl.ds(8, C), :]))
    propagate(coef, 0, sc, sb, 4, 8, into(sa, lambda i: hold[8 + i, pl.ds(8, C), :]))
    propagate(coef, 0, sa, sb, 4, 8, into(sc, lambda i: f2[i]))
    propagate(coef, 0, sc, sb, 4, 8,
              into(rp, lambda i: f3[i] - (hold[1 + i, pl.ds(8, C), :] if i < 3 else g3[...])))

    span = pl.ds(Z, W)

    def single(m, src, dst, term):
        def emit(at, x):
            dst[span, :] = x if term is None else x + term()
        propagate(coef, m, src, lb, 0, H, emit)

    single(1, rp.at[0], la, lambda: rp[1, span, :])
    single(1, la, lc, lambda: rp[2, span, :])
    single(1, lc, y2, lambda: rp[3, span, :])

    halo_r = both(7, rp.at[pl.ds(0, 3), pl.ds(Z + C, 24), :], rsl,
                  rp.at[pl.ds(0, 3), pl.ds(Z + H - 8, 24), :], rsr)

    hand = pltpu.make_async_remote_copy(src_ref=y2.at[span, :], dst_ref=y1p.at[span, :], send_sem=ssem.at[9],
                                        recv_sem=rsem.at[9], device_id=(tm, 1, c), device_id_type=MESH)

    @pl.when(sx == 0)
    def _():
        hand.start()
        y1[...] = y2[span, :]

    @pl.when(sx == 1)
    def _():
        hand.wait_recv()
        y1[...] = y1p[span, :]

    @pl.when(place == 1)
    def _():
        single(2, y1p, e1p, lambda: y2[span, :])
        yl[...] = e1p[span, :]

    @pl.when(place != 1)
    def _():
        yl[...] = y2[span, :]

    edge_1 = both(10, y1.at[pl.ds(C, 2 * H), :], rl.at[0], y1.at[pl.ds(0, 2 * H), :], rr.at[0])
    edge_2 = both(12, yl.at[pl.ds(C, 2 * H), :], rl.at[1], yl.at[pl.ds(0, 2 * H), :], rr.at[1])

    def joined(dst, own, from_left, from_right):
        dst[pl.ds(Z, 2 * H), :] = own[pl.ds(0, 2 * H), :] + has_left * from_left[...]
        dst[pl.ds(Z + 2 * H, C - 2 * H), :] = own[pl.ds(2 * H, C - 2 * H), :]
        dst[pl.ds(Z + C, 2 * H), :] = own[pl.ds(C, 2 * H), :] + has_right * from_right[...]

    arrive(*edge_2)
    joined(y2f, yl, rl.at[1], rr.at[1])

    cross = [
        pltpu.make_async_remote_copy(src_ref=y2f.at[span, :], dst_ref=e1.at[span, :], send_sem=ssem.at[14 + s],
                                     recv_sem=rsem.at[14], device_id=(1, s, c), device_id_type=MESH)
        for s in range(2)
    ]

    @pl.when(place == 1)
    def _():
        cross[1].start()
        cross[0].start()

    arrive(*edge_1)
    joined(y1f, y1, rl.at[0], rr.at[0])

    arrive(*halo_r)
    for i in range(3):
        rf[i, pl.ds(Z, 24), :] = rp[i, pl.ds(Z, 24), :] + has_left * rsl[i]
        rf[i, pl.ds(Z + 24, W - 48), :] = rp[i, pl.ds(Z + 24, W - 48), :]
        rf[i, pl.ds(Z + W - 24, 24), :] = rp[i, pl.ds(Z + W - 24, 24), :] + has_right * rsr[i]

    @pl.when(place == 0)
    def _():
        yr[...] = y1f[main, :]

    @pl.when(place == 1)
    def _():
        bf[span, :] = y1f[span, :]
        yr[...] = y2f[main, :]

    @pl.when(tm == 1)
    def _():
        cross[0].wait_recv()

    @pl.when(place == 2)
    def _():
        bf[span, :] = e1[span, :]
        single(2, bf, la, lambda: y1f[span, :])
        yr[...] = la[main, :]

    @pl.when(place == 3)
    def _():
        single(2, e1, bf, lambda: y1f[span, :])
        single(2, bf, la, lambda: y2f[span, :])
        yr[...] = la[main, :]

    arrive(*halo_h, *halo_s)

    def halo(i):
        return has_left * hold[i, pl.ds(0, 8), :], hold[i, pl.ds(8, C), :], has_right * hold[i, pl.ds(8 + C, 8), :]

    low, mid, high = pl.ds(Z + H - 8, 8), main, pl.ds(Z + H + C, 8)

    def begin(i, e):
        a, b, d = halo(i)
        sa[i, low, :] = a + e[low, :]
        if i:
            b = b + e[mid, :]
            out[4 * i - 1] = b.T
            sa[i, mid, :] = b
        else:
            sa[i, mid, :] = b + e[mid, :]
        sa[i, high, :] = d + e[high, :]

    begin(0, bf)
    single(1, bf, la, lambda: rf[0, span, :])
    begin(1, la)
    single(1, la, lc, lambda: rf[1, span, :])
    begin(2, lc)
    single(1, lc, la, lambda: rf[2, span, :])
    begin(3, la)
    out[15] = (g3[...] + yr[...]).T

    def relaxed(dst, first, step):
        def emit(at, x):
            a, b, d = halo(first + at[0])
            b = x[8 : 8 + C] + b
            out[4 * at[0] + step] = b.T
            dst[at + (low,)] = x[:8] + a
            dst[at + (mid,)] = b
            dst[at + (high,)] = x[8 + C :] + d
        return emit

    def last(at, x):
        out[4 * at[0] + 2] = (x + f2[at[0]]).T

    propagate(coef, 0, sa, sb, 4, 8, relaxed(sc, 4, 0))
    propagate(coef, 0, sc, sb, 4, 8, relaxed(sa, 8, 1))

    def final(at, x):
        last(at, x[8 : 8 + C])

    propagate(coef, 0, sa, sb, 4, 8, final)

    for copy in sent:
        copy.wait_send()

    @pl.when(place < 3)
    def _():
        prev_copy.wait_send()

    @pl.when(sx == 0)
    def _():
        hand.wait_send()

    @pl.when(place == 1)
    def _():
        cross[0].wait_send()
        cross[1].wait_send()


def local(u_init, guess, forcing, speed_x, speed_y, diffusion):
    def vmem(*shape):
        return pltpu.VMEM(shape, F32)

    any_space = pl.BlockSpec(memory_space=pltpu.HBM)
    field = (N, C)
    return pl.pallas_call(
        kernel,
        out_shape=jax.ShapeDtypeStruct(forcing.shape, F32),
        in_specs=[any_space] * 6,
        out_specs=pl.BlockSpec(memory_space=pltpu.VMEM),
        scratch_shapes=[
            vmem(3, C, C), vmem(C, C), vmem(4, C, C), vmem(16, C, C), vmem(C, C),
            vmem(3, W, C), vmem(3, 5, W, C),
            vmem(12, C + 16, C), vmem(C, C), vmem(4, C, C), vmem(4, C, C),
            vmem(4, *field), vmem(4, *field), vmem(4, *field), vmem(4, *field), vmem(3, *field),
            vmem(*field), vmem(*field), vmem(*field),
            vmem(*field), vmem(W, C), vmem(*field), vmem(*field), vmem(*field),
            vmem(*field), vmem(*field), vmem(*field),
            vmem(2, 2 * H, C), vmem(2, 2 * H, C), vmem(W, C), vmem(C, C),
            vmem(3, 24, C), vmem(3, 24, C),
            pltpu.SemaphoreType.DMA((6,)),
            pltpu.SemaphoreType.DMA((16,)),
            pltpu.SemaphoreType.DMA((16,)),
        ],
        compiler_params=pltpu.CompilerParams(collective_id=0, has_side_effects=True, vmem_limit_bytes=60 << 20),
    )(u_init, guess, forcing, speed_x, speed_y, diffusion)


def solution(mesh):
    placed = (
        P(None, "sy"),
        P(("tm", "sx"), None, "sy"),
        P(("tm", "sx"), None, "sy"),
        P(None, "sy"),
        P(None, "sy"),
        P(None, "sy"),
    )
    return jax.shard_map(
        local, mesh=mesh, in_specs=placed, out_specs=P(("tm", "sx"), None, "sy"), check_vma=False
    )
```

time: 558 us -> 30.8 us (0.06)
  the two profiles are of different devices: /device:TPU:132 before, /device:TPU:4 now
where the time goes in v1:
time: 30.8 us; the launch traced here: 30.7 us
  Pallas kernels  28.4 us (92%)
  local copies, waits for them, and re-layouts  2.3 us (7%)
    pallas_call x1, Pallas kernels, local(): pl.pallas_call(kernel, out_shape=jax.ShapeDtypeStruct(forcing.shape, F32)...  28.4 us
    unnamed x1, local copies, waits for them, and re-layouts  2.3 us

profile of v1, /device:TPU:4, one launch (start us, length us, event | category | flops | bytes accessed | tf_op | source)
XLA Modules:
  0.0 30.7 jit_solution(11038918743544264661)
XLA Ops:
  0.0 28.4 %shard_map.64 = f32[16,128,128]{2,1,0:T(8,128)} custom-call(f32[128,128]{1,0:T(8,128)} %u_hbm.1, f32[4,128,128]{2,1,0:T(8,128)} %guess_hbm.1, f32[16,128,128]{2,1,0:T(8,128)} %forcing_hbm.1, f32[128,128]{1,0:T(8,128)} %sx_hbm.1, f32[128,128]{1,0:T(8,128)} %sy_hbm.1, f32[128,128]{1,0:T(8,128)} %d_hbm.1), custom_call_target="tpu_custom_call" | custom-call | tf_op jit(solution)/shard_map/pallas_call | solution.py:349
  28.4 2.3 %copy.8 = f32[16,128,128]{2,1,0:T(8,128)} copy(f32[16,128,128]{2,1,0:T(8,128)} %shard_map.64) | data formatting | bytes 2097152

commit v2 on v1

--- a/solution.py
+++ b/solution.py
@@ -46,9 +46,7 @@
     tm, sx, c = lax.axis_index("tm"), lax.axis_index("sx"), lax.axis_index("sy")
     count = lax.axis_size("sy")
     place = 2 * tm + sx
-    right, left = lax.rem(c + 1, count), lax.rem(c + count - 1, count)
-    has_left = jnp.where(c > 0, 1.0, 0.0).astype(F32)
-    has_right = jnp.where(c < count - 1, 1.0, 0.0).astype(F32)
+    has_left, has_right = c > 0, c < count - 1
 
     def fetch(src, dst, i):
         copy = pltpu.make_async_copy(src, dst, lsem.at[i])
@@ -65,8 +63,14 @@
     def greet(*device):
         pl.semaphore_signal(barrier, inc=1, device_id=device, device_id_type=MESH)
 
-    greet(tm, sx, left)
-    greet(tm, sx, right)
+    @pl.when(has_left)
+    def _():
+        greet(tm, sx, c - 1)
+
+    @pl.when(has_right)
+    def _():
+        greet(tm, sx, c + 1)
+
     greet(tm, 1 - sx, c)
 
     @pl.when(place == 1)
@@ -84,28 +88,42 @@
         ref[pl.ds(0, Z), :] = jnp.zeros((Z, ref.shape[1]), F32)
         ref[pl.ds(N - Z, Z), :] = jnp.zeros((Z, ref.shape[1]), F32)
 
+    @pl.when(c == 0)
+    def _():
+        kraw[:, pl.ds(0, H), :] = jnp.zeros((3, H, C), F32)
+        hold[:, pl.ds(0, 8), :] = jnp.zeros((12, 8, C), F32)
+        rl[...] = jnp.zeros_like(rl)
+        rsl[...] = jnp.zeros_like(rsl)
+
+    @pl.when(c == count - 1)
+    def _():
+        kraw[:, pl.ds(H + C, H), :] = jnp.zeros((3, H, C), F32)
+        hold[:, pl.ds(8 + C, 8), :] = jnp.zeros((12, 8, C), F32)
+        rr[...] = jnp.zeros_like(rr)
+        rsr[...] = jnp.zeros_like(rsr)
+
     for i, load in enumerate(loads_k):
         load.wait()
         kraw[i, pl.ds(H, C), :] = raw_k[i].T
 
-    pl.semaphore_wait(barrier, jnp.where(place == 1, 5, 3 + tm))
+    pl.semaphore_wait(barrier, jnp.where(place == 1, 3, 1 + tm) + jnp.where(has_left, 1, 0) + jnp.where(has_right, 1, 0))
 
     sent = []
 
-    def send(i, src, dst, device):
-        copy = pltpu.make_async_remote_copy(src_ref=src, dst_ref=dst, send_sem=ssem.at[i], recv_sem=rsem.at[i],
+    def copy_of(i, src, dst, *device):
+        return pltpu.make_async_remote_copy(src_ref=src, dst_ref=dst, send_sem=ssem.at[i], recv_sem=rsem.at[i],
                                             device_id=device, device_id_type=MESH)
-        copy.start()
-        return copy
 
     def both(i, to_right, at_right, to_left, at_left):
-        pair = (send(i, to_right, at_right, (tm, sx, right)), send(i + 1, to_left, at_left, (tm, sx, left)))
-        sent.extend(pair)
-        return pair
-
-    def arrive(*copies):
-        for copy in copies:
-            copy.wait_recv()
+        up, down = copy_of(i, to_right, at_right, tm, sx, c + 1), copy_of(i + 1, to_left, at_left, tm, sx, c - 1)
+        pl.when(has_right)(up.start)
+        pl.when(has_left)(down.start)
+        sent.append((up, down))
+        return up, down
+
+    def arrive(up, down):
+        pl.when(has_left)(up.wait_recv)
+        pl.when(has_right)(down.wait_recv)
 
     halo_k = both(0, kraw.at[:, pl.ds(C, H), :], kraw.at[:, pl.ds(0, H), :],
                   kraw.at[:, pl.ds(H, H), :], kraw.at[:, pl.ds(H + C, H), :])
@@ -113,8 +131,7 @@
     load_g.wait()
     after = place + 1
     onward = (lax.div(after, 2), lax.rem(after, 2), c)
-    prev_copy = pltpu.make_async_remote_copy(src_ref=raw_g.at[3], dst_ref=prev, send_sem=ssem.at[2], recv_sem=rsem.at[2],
-                                             device_id=onward, device_id_type=MESH)
+    prev_copy = copy_of(2, raw_g.at[3], prev, *onward)
 
     @pl.when(place < 3)
     def _():
@@ -148,9 +165,7 @@
 
     arrive(*halo_k)
     row = lax.broadcasted_iota(jnp.int32, (W, C), 1)
-    column = lax.broadcasted_iota(jnp.int32, (W, C), 0)
-    inside = jnp.where(column < H, has_left, jnp.where(column >= H + C, has_right, 1.0))
-    speed_x, speed_y, diffusion = kraw[0] * inside, kraw[1] * inside, kraw[2] * inside
+    speed_x, speed_y, diffusion = kraw[0], kraw[1], kraw[2]
     west = jnp.maximum(speed_x, 0.0) + diffusion
     east = diffusion - jnp.minimum(speed_x, 0.0)
     south = jnp.maximum(speed_y, 0.0) + diffusion
@@ -197,8 +212,7 @@
     halo_r = both(7, rp.at[pl.ds(0, 3), pl.ds(Z + C, 24), :], rsl,
                   rp.at[pl.ds(0, 3), pl.ds(Z + H - 8, 24), :], rsr)
 
-    hand = pltpu.make_async_remote_copy(src_ref=y2.at[span, :], dst_ref=y1p.at[span, :], send_sem=ssem.at[9],
-                                        recv_sem=rsem.at[9], device_id=(tm, 1, c), device_id_type=MESH)
+    hand = copy_of(9, y2.at[span, :], y1p.at[span, :], tm, 1, c)
 
     @pl.when(sx == 0)
     def _():
@@ -223,9 +237,9 @@
     edge_2 = both(12, yl.at[pl.ds(C, 2 * H), :], rl.at[1], yl.at[pl.ds(0, 2 * H), :], rr.at[1])
 
     def joined(dst, own, from_left, from_right):
-        dst[pl.ds(Z, 2 * H), :] = own[pl.ds(0, 2 * H), :] + has_left * from_left[...]
+        dst[pl.ds(Z, 2 * H), :] = own[pl.ds(0, 2 * H), :] + from_left[...]
         dst[pl.ds(Z + 2 * H, C - 2 * H), :] = own[pl.ds(2 * H, C - 2 * H), :]
-        dst[pl.ds(Z + C, 2 * H), :] = own[pl.ds(C, 2 * H), :] + has_right * from_right[...]
+        dst[pl.ds(Z + C, 2 * H), :] = own[pl.ds(C, 2 * H), :] + from_right[...]
 
     arrive(*edge_2)
     joined(y2f, yl, rl.at[1], rr.at[1])
@@ -246,9 +260,9 @@
 
     arrive(*halo_r)
     for i in range(3):
-        rf[i, pl.ds(Z, 24), :] = rp[i, pl.ds(Z, 24), :] + has_left * rsl[i]
+        rf[i, pl.ds(Z, 24), :] = rp[i, pl.ds(Z, 24), :] + rsl[i]
         rf[i, pl.ds(Z + 24, W - 48), :] = rp[i, pl.ds(Z + 24, W - 48), :]
-        rf[i, pl.ds(Z + W - 24, 24), :] = rp[i, pl.ds(Z + W - 24, 24), :] + has_right * rsr[i]
+        rf[i, pl.ds(Z + W - 24, 24), :] = rp[i, pl.ds(Z + W - 24, 24), :] + rsr[i]
 
     @pl.when(place == 0)
     def _():
@@ -275,10 +289,11 @@
         single(2, bf, la, lambda: y2f[span, :])
         yr[...] = la[main, :]
 
-    arrive(*halo_h, *halo_s)
+    arrive(*halo_h)
+    arrive(*halo_s)
 
     def halo(i):
-        return has_left * hold[i, pl.ds(0, 8), :], hold[i, pl.ds(8, C), :], has_right * hold[i, pl.ds(8 + C, 8), :]
+        return hold[i, pl.ds(0, 8), :], hold[i, pl.ds(8, C), :], hold[i, pl.ds(8 + C, 8), :]
 
     low, mid, high = pl.ds(Z + H - 8, 8), main, pl.ds(Z + H + C, 8)
 
@@ -323,8 +338,9 @@
 
     propagate(coef, 0, sa, sb, 4, 8, final)
 
-    for copy in sent:
-        copy.wait_send()
+    for up, down in sent:
+        pl.when(has_right)(up.wait_send)
+        pl.when(has_left)(down.wait_send)
 
     @pl.when(place < 3)
     def _():
@@ -348,7 +364,7 @@
     field = (N, C)
     return pl.pallas_call(
         kernel,
-        out_shape=jax.ShapeDtypeStruct(forcing.shape, F32),
+        out_shape=pltpu.VMEM(forcing.shape, F32),
         in_specs=[any_space] * 6,
         out_specs=pl.BlockSpec(memory_space=pltpu.VMEM),
         scratch_shapes=[

time: 30.8 us -> 22.9 us (0.74)
  the two profiles are of different devices: /device:TPU:4 before, /device:TPU:132 now
where the time goes in v2:
time: 22.9 us; the launch traced here: 22.7 us
  Pallas kernels  21.7 us (95%)
  local copies, waits for them, and re-layouts  0.97 us (4%)
    pallas_call x1, Pallas kernels, local(): pl.pallas_call(kernel, out_shape=pltpu.VMEM(forcing.shape, F32), in_specs...  21.7 us
    unnamed x1, local copies, waits for them, and re-layouts  0.97 us

profile of v2, /device:TPU:132, one launch (start us, length us, event | category | flops | bytes accessed | tf_op | source)
XLA Modules:
  0.0 22.7 jit_solution(495537191672382978)
XLA Ops:
  0.0 21.7 %shard_map.64 = f32[16,128,128]{2,1,0:T(8,128)S(1)} custom-call(f32[128,128]{1,0:T(8,128)} %u_hbm.1, f32[4,128,128]{2,1,0:T(8,128)} %guess_hbm.1, f32[16,128,128]{2,1,0:T(8,128)} %forcing_hbm.1, f32[128,128]{1,0:T(8,128)} %sx_hbm.1, f32[128,128]{1,0:T(8,128)} %sy_hbm.1, f32[128,128]{1,0:T(8,128)} %d_hbm.1), custom_call_target="tpu_custom_call" | custom-call | tf_op jit(solution)/shard_map/pallas_call | solution.py:365
  21.7 1.0 %copy.8 = f32[16,128,128]{2,1,0:T(8,128)} copy(f32[16,128,128]{2,1,0:T(8,128)S(1)} %shard_map.64) | data formatting | bytes 2097152

commit v3 on v2

--- a/solution.py
+++ b/solution.py
@@ -41,12 +41,13 @@
 
 def kernel(u_hbm, guess_hbm, forcing_hbm, sx_hbm, sy_hbm, d_hbm, out,
            raw_k, raw_u, raw_g, raw_f, prev, kraw, coef, hold, g3, f2, f3, sa, sb, sc, rp, rf,
-           la, lb, lc, y1p, y1, y2, y1f, y2f, e1p, e1, bf, rl, rr, yl, yr, rsl, rsr,
+           la, lb, lc, y1p, y1, y2, y1f, y2f, e1p, e1, bf, em, el, er, rl, rr, yl, yr, rsl, rsr,
            lsem, ssem, rsem):
     tm, sx, c = lax.axis_index("tm"), lax.axis_index("sx"), lax.axis_index("sy")
     count = lax.axis_size("sy")
     place = 2 * tm + sx
     has_left, has_right = c > 0, c < count - 1
+    left, right = lax.rem(c + count - 1, count), lax.rem(c + 1, count)
 
     def fetch(src, dst, i):
         copy = pltpu.make_async_copy(src, dst, lsem.at[i])
@@ -94,6 +95,7 @@
         hold[:, pl.ds(0, 8), :] = jnp.zeros((12, 8, C), F32)
         rl[...] = jnp.zeros_like(rl)
         rsl[...] = jnp.zeros_like(rsl)
+        el[...] = jnp.zeros_like(el)
 
     @pl.when(c == count - 1)
     def _():
@@ -101,6 +103,7 @@
         hold[:, pl.ds(8 + C, 8), :] = jnp.zeros((12, 8, C), F32)
         rr[...] = jnp.zeros_like(rr)
         rsr[...] = jnp.zeros_like(rsr)
+        er[...] = jnp.zeros_like(er)
 
     for i, load in enumerate(loads_k):
         load.wait()
@@ -110,12 +113,12 @@
 
     sent = []
 
-    def copy_of(i, src, dst, *device):
-        return pltpu.make_async_remote_copy(src_ref=src, dst_ref=dst, send_sem=ssem.at[i], recv_sem=rsem.at[i],
+    def copy_of(i, src, dst, *device, at=None):
+        return pltpu.make_async_remote_copy(src_ref=src, dst_ref=dst, send_sem=ssem.at[i], recv_sem=rsem.at[i if at is None else at],
                                             device_id=device, device_id_type=MESH)
 
     def both(i, to_right, at_right, to_left, at_left):
-        up, down = copy_of(i, to_right, at_right, tm, sx, c + 1), copy_of(i + 1, to_left, at_left, tm, sx, c - 1)
+        up, down = copy_of(i, to_right, at_right, tm, sx, right), copy_of(i + 1, to_left, at_left, tm, sx, left)
         pl.when(has_right)(up.start)
         pl.when(has_left)(down.start)
         sent.append((up, down))
@@ -224,9 +227,17 @@
         hand.wait_recv()
         y1[...] = y1p[span, :]
 
+    cross = []
+    for s in (1, 0):
+        cross.append((has_right, copy_of(16 + s, e1p.at[pl.ds(Z + C, 2 * H), :], el, 1, s, right, at=16)))
+        cross.append((has_left, copy_of(18 + s, e1p.at[pl.ds(Z, 2 * H), :], er, 1, s, left, at=17)))
+        cross.append((None, copy_of(14 + s, e1p.at[span, :], em, 1, s, c, at=14)))
+
     @pl.when(place == 1)
     def _():
         single(2, y1p, e1p, lambda: y2[span, :])
+        for condition, copy in cross:
+            copy.start() if condition is None else pl.when(condition)(copy.start)
         yl[...] = e1p[span, :]
 
     @pl.when(place != 1)
@@ -243,17 +254,6 @@
 
     arrive(*edge_2)
     joined(y2f, yl, rl.at[1], rr.at[1])
-
-    cross = [
-        pltpu.make_async_remote_copy(src_ref=y2f.at[span, :], dst_ref=e1.at[span, :], send_sem=ssem.at[14 + s],
-                                     recv_sem=rsem.at[14], device_id=(1, s, c), device_id_type=MESH)
-        for s in range(2)
-    ]
-
-    @pl.when(place == 1)
-    def _():
-        cross[1].start()
-        cross[0].start()
 
     arrive(*edge_1)
     joined(y1f, y1, rl.at[0], rr.at[0])
@@ -264,30 +264,26 @@
         rf[i, pl.ds(Z + 24, W - 48), :] = rp[i, pl.ds(Z + 24, W - 48), :]
         rf[i, pl.ds(Z + W - 24, 24), :] = rp[i, pl.ds(Z + W - 24, 24), :] + rsr[i]
 
-    @pl.when(place == 0)
-    def _():
-        yr[...] = y1f[main, :]
+    yr[...] = jnp.where(sx == 0, y1f[main, :], y2f[main, :])
 
     @pl.when(place == 1)
     def _():
         bf[span, :] = y1f[span, :]
-        yr[...] = y2f[main, :]
 
     @pl.when(tm == 1)
     def _():
-        cross[0].wait_recv()
+        cross[2][1].wait_recv()
+        pl.when(has_left)(cross[0][1].wait_recv)
+        pl.when(has_right)(cross[1][1].wait_recv)
 
     @pl.when(place == 2)
     def _():
-        bf[span, :] = e1[span, :]
-        single(2, bf, la, lambda: y1f[span, :])
-        yr[...] = la[main, :]
+        joined(bf, em, el, er)
 
     @pl.when(place == 3)
     def _():
+        joined(e1, em, el, er)
         single(2, e1, bf, lambda: y1f[span, :])
-        single(2, bf, la, lambda: y2f[span, :])
-        yr[...] = la[main, :]
 
     arrive(*halo_h)
     arrive(*halo_s)
@@ -315,7 +311,10 @@
     begin(2, lc)
     single(1, lc, la, lambda: rf[2, span, :])
     begin(3, la)
-    out[15] = (g3[...] + yr[...]).T
+
+    def owned(at, x):
+        out[15] = (g3[...] + (yr[...] + jnp.where(place == 1, 0.0, x[8 : 8 + C]))).T
+
 
     def relaxed(dst, first, step):
         def emit(at, x):
@@ -337,6 +336,7 @@
         last(at, x[8 : 8 + C])
 
     propagate(coef, 0, sa, sb, 4, 8, final)
+    propagate(coef, 2, bf, lb, 0, 8, owned)
 
     for up, down in sent:
         pl.when(has_right)(up.wait_send)
@@ -352,8 +352,8 @@
 
     @pl.when(place == 1)
     def _():
-        cross[0].wait_send()
-        cross[1].wait_send()
+        for condition, copy in cross:
+            copy.wait_send() if condition is None else pl.when(condition)(copy.wait_send)
 
 
 def local(u_init, guess, forcing, speed_x, speed_y, diffusion):
@@ -375,11 +375,12 @@
             vmem(*field), vmem(*field), vmem(*field),
             vmem(*field), vmem(W, C), vmem(*field), vmem(*field), vmem(*field),
             vmem(*field), vmem(*field), vmem(*field),
+            vmem(W, C), vmem(2 * H, C), vmem(2 * H, C),
             vmem(2, 2 * H, C), vmem(2, 2 * H, C), vmem(W, C), vmem(C, C),
             vmem(3, 24, C), vmem(3, 24, C),
             pltpu.SemaphoreType.DMA((6,)),
-            pltpu.SemaphoreType.DMA((16,)),
-            pltpu.SemaphoreType.DMA((16,)),
+            pltpu.SemaphoreType.DMA((20,)),
+            pltpu.SemaphoreType.DMA((20,)),
         ],
         compiler_params=pltpu.CompilerParams(collective_id=0, has_side_effects=True, vmem_limit_bytes=60 << 20),
     )(u_init, guess, forcing, speed_x, speed_y, diffusion)

time: 22.9 us -> 20.6 us (0.90)
  the two profiles are of different devices: /device:TPU:132 before, /device:TPU:161 now
where the time goes in v3:
time: 20.6 us; the launch traced here: 20.5 us
  Pallas kernels  19.5 us (95%)
  local copies, waits for them, and re-layouts  0.97 us (5%)
    pallas_call x1, Pallas kernels, local(): pl.pallas_call(kernel, out_shape=pltpu.VMEM(forcing.shape, F32), in_specs...  19.5 us
    unnamed x1, local copies, waits for them, and re-layouts  0.97 us

profile of v3, /device:TPU:161, one launch (start us, length us, event | category | flops | bytes accessed | tf_op | source)
XLA Modules:
  0.0 20.5 jit_solution(214480764927548040)
XLA Ops:
  0.0 19.5 %shard_map.64 = f32[16,128,128]{2,1,0:T(8,128)S(1)} custom-call(f32[128,128]{1,0:T(8,128)} %u_hbm.1, f32[4,128,128]{2,1,0:T(8,128)} %guess_hbm.1, f32[16,128,128]{2,1,0:T(8,128)} %forcing_hbm.1, f32[128,128]{1,0:T(8,128)} %sx_hbm.1, f32[128,128]{1,0:T(8,128)} %sy_hbm.1, f32[128,128]{1,0:T(8,128)} %d_hbm.1), custom_call_target="tpu_custom_call" | custom-call | tf_op jit(solution)/shard_map/pallas_call | solution.py:365
  19.5 1.0 %copy.8 = f32[16,128,128]{2,1,0:T(8,128)} copy(f32[16,128,128]{2,1,0:T(8,128)S(1)} %shard_map.64) | data formatting | bytes 2097152

commit v4 on v3

v4 whole, which is shorter than its diff:
```python
import functools

import jax
import jax.numpy as jnp
from jax import lax
from jax.experimental import pallas as pl
from jax.experimental.pallas import tpu as pltpu
from jax.sharding import PartitionSpec as P

MESH = pl.DeviceIdType.MESH
C = 128
H = 16
W = C + 2 * H
Z = 8
N = W + 2 * Z
F32 = jnp.float32


def west_of(x):
    return pltpu.roll(x, 1, 1)


def east_of(x):
    return pltpu.roll(x, C - 1, 1)


def build(base, coef, lo, n):
    def at(j, shift):
        return base[j, pl.ds(lo + shift, n), :]

    w, e, s, n_, c = (at(j, 0) for j in range(5))
    ww, we, ws, wn, wc = (west_of(x) for x in (w, e, s, n_, c))
    ew, ee, es, en, ec = (east_of(x) for x in (w, e, s, n_, c))
    loop = (w * we + e * ew) + (s * at(3, -1) + n_ * at(2, 1))
    centre = 0.5 * (c * c + loop)
    to_west = -0.5 * w * (c + wc)
    to_east = -0.5 * e * (c + ec)
    to_south = -0.5 * s * (c + at(4, -1))
    to_north = -0.5 * n_ * (c + at(4, 1))
    west_south = 0.5 * (w * ws + s * at(0, -1))
    west_north = 0.5 * (w * wn + n_ * at(0, 1))
    east_south = 0.5 * (e * es + s * at(1, -1))
    east_north = 0.5 * (e * en + n_ * at(1, 1))
    linear = (-c, s, n_, ew, we)
    square = (centre, to_south, to_north, east_of(to_west), west_of(to_east))
    rest = (0.5 * s * at(2, -1), 0.5 * n_ * at(3, 1), 0.5 * w * ww, 0.5 * e * ee,
            east_of(west_south), east_of(west_north), west_of(east_south), west_of(east_north))
    rows = pl.ds(lo - Z, n)
    for m, factor in enumerate((1.0, 4.0, 16.0)):
        for j in range(5):
            term = factor * linear[j] + (factor * factor) * square[j]
            coef[m, j, rows, :] = 1.0 + term if j == 0 else term
        for j in range(8):
            coef[m, 5 + j, rows, :] = (factor * factor) * rest[j]


def heun(coef, m, src, at, lo, n):
    def field(shift):
        return src[at + (pl.ds(lo + shift, n),)]

    def k(j):
        return coef[m, j, pl.ds(lo - Z, n), :]

    v, south, north = field(0), field(-1), field(1)
    from_west = k(3) * v + k(9) * south + k(10) * north
    from_east = k(4) * v + k(11) * south + k(12) * north
    columns = (k(0) * v + k(1) * south) + (k(2) * north + k(5) * field(-2)) + k(6) * field(2)
    rows = k(7) * pltpu.roll(v, 2, 1) + k(8) * pltpu.roll(v, C - 2, 1)
    return (columns + rows) + (west_of(from_west) + east_of(from_east))


def kernel(u_hbm, guess_hbm, forcing_hbm, sx_hbm, sy_hbm, d_hbm, out,
           raw_k, raw_u, raw_g, raw_f, prev, kraw, base, coef, hold, g3, f2, f3, sa, sb, sc, sd, rp, rf,
           la, lb, lc, y1p, y1, y2, y1f, y2f, e1p, e1, bf, em, el, er, rl, rr, rl2, rr2, yl, rsl, rsr, to_left, to_right, from_left, from_right,
           lsem, ssem, rsem, k_sem):
    tm, sx, c = lax.axis_index("tm"), lax.axis_index("sx"), lax.axis_index("sy")
    count = lax.axis_size("sy")
    place = 2 * tm + sx
    has_left, has_right = c > 0, c < count - 1
    left, right = lax.rem(c + count - 1, count), lax.rem(c + 1, count)

    def fetch(src, dst, i):
        copy = pltpu.make_async_copy(src, dst, lsem.at[i])
        copy.start()
        return copy

    loads_k = [fetch(ref, raw_k.at[i], i) for i, ref in enumerate((sx_hbm, sy_hbm, d_hbm))]
    load_g = fetch(guess_hbm, raw_g, 3)
    load_u = fetch(u_hbm, raw_u, 4)
    load_f = fetch(forcing_hbm, raw_f, 5)

    teller = (tm == 1) | (sx == 0)
    barrier = pltpu.get_barrier_semaphore()

    def greet(*device):
        pl.semaphore_signal(barrier, inc=1, device_id=device, device_id_type=MESH)

    @pl.when(has_left)
    def _():
        greet(tm, tm * sx, left)

    @pl.when(has_right)
    def _():
        greet(tm, tm * sx, right)

    greet(tm, 1 - sx, c)

    @pl.when(tm == 1)
    def _():
        greet(0, 0, c)
        greet(0, 1, c)

    for ref in (sa, sb, sc, sd, rp, rf, la, lb, lc, bf, base):
        ref[...] = jnp.zeros_like(ref)
    for ref in (y1p, y1f, y2, e1p, e1):
        ref[pl.ds(0, Z), :] = jnp.zeros((Z, ref.shape[1]), F32)
        ref[pl.ds(N - Z, Z), :] = jnp.zeros((Z, ref.shape[1]), F32)

    hold[:, pl.ds(0, 8), :] = jnp.zeros((12, 8, C), F32)
    hold[:, pl.ds(8 + C, 8), :] = jnp.zeros((12, 8, C), F32)

    @pl.when(c == 0)
    def _():
        kraw[:, pl.ds(0, H), :] = jnp.zeros((3, H, C), F32)
        from_left[...] = jnp.zeros_like(from_left)
        rl[...] = jnp.zeros_like(rl)
        rsl[...] = jnp.zeros_like(rsl)
        el[...] = jnp.zeros_like(el)

    @pl.when(c == count - 1)
    def _():
        kraw[:, pl.ds(H + C, H), :] = jnp.zeros((3, H, C), F32)
        from_right[...] = jnp.zeros_like(from_right)
        rr[...] = jnp.zeros_like(rr)
        rsr[...] = jnp.zeros_like(rsr)
        er[...] = jnp.zeros_like(er)

    for i, load in enumerate(loads_k):
        load.wait()
        kraw[i, pl.ds(H, C), :] = raw_k[i].T

    sides = jnp.where(has_left, 1, 0) + jnp.where(has_right, 1, 0)
    pl.semaphore_wait(barrier, 1 + jnp.where(tm == 0, 2 + 2 * (1 - sx) * sides, sides))

    sent = []

    def make_copy(src, dst, send_sem, recv_sem, *device):
        return pltpu.make_async_remote_copy(src_ref=src, dst_ref=dst, send_sem=send_sem, recv_sem=recv_sem,
                                            device_id=device, device_id_type=MESH)

    def copy_of(i, src, dst, *device, at=None):
        return make_copy(src, dst, ssem.at[i], rsem.at[i if at is None else at], *device)

    def pair(i, to_right, at_right, to_left, at_left):
        sent.append((copy_of(i, to_right, at_right, tm, sx, right), copy_of(i + 1, to_left, at_left, tm, sx, left)))
        return sent[-1]

    def tell(copies):
        pl.when(has_right)(copies[0].start)
        pl.when(has_left)(copies[1].start)

    def both(*what):
        copies = pair(*what)
        tell(copies)
        return copies

    def arrive(up, down):
        pl.when(has_left)(up.wait_recv)
        pl.when(has_right)(down.wait_recv)

    halo_k = []
    for i, to, told in ((0, tm * sx, teller), (2, 1, place == 0)):
        up = make_copy(kraw.at[:, pl.ds(C, H), :], kraw.at[:, pl.ds(0, H), :], k_sem.at[i], rsem.at[0], tm, to, right)
        down = make_copy(kraw.at[:, pl.ds(H, H), :], kraw.at[:, pl.ds(H + C, H), :], k_sem.at[i + 1], rsem.at[1],
                         tm, to, left)
        pl.when(told & has_right)(up.start)
        pl.when(told & has_left)(down.start)
        halo_k.append((up, down, told))

    load_g.wait()
    after = place + 1
    onward = (lax.div(after, 2), lax.rem(after, 2), c)
    prev_copy = copy_of(2, raw_g.at[3], prev, *onward)

    @pl.when(place < 3)
    def _():
        prev_copy.start()

    for i in range(3):
        hold[1 + i, pl.ds(8, C), :] = raw_g[i].T
    g3[...] = raw_g[3].T
    load_u.wait()
    load_f.wait()
    for j in range(4):
        hold[4 + j, pl.ds(8, C), :] = raw_f[4 * j].T
        hold[8 + j, pl.ds(8, C), :] = raw_f[4 * j + 1].T
    for i in range(4):
        to_right[i, pl.ds(6, 2), :] = hold[8 + i, pl.ds(8 + C - 2, 2), :]
        to_left[i, pl.ds(6, 2), :] = hold[8 + i, pl.ds(8, 2), :]
        to_right[4 + i // 2, pl.ds(4 * (i % 2), 4), :] = hold[4 + i, pl.ds(8 + C - 4, 4), :]
        to_left[4 + i // 2, pl.ds(4 * (i % 2), 4), :] = hold[4 + i, pl.ds(8, 4), :]
    for i in range(1, 4):
        to_right[i, pl.ds(0, 6), :] = hold[i, pl.ds(8 + C - 6, 6), :]
        to_left[i, pl.ds(0, 6), :] = hold[i, pl.ds(8, 6), :]
    tiles = pl.ds(1, 5)
    halo_h = pair(3, to_right.at[tiles], from_left.at[tiles], to_left.at[tiles], from_right.at[tiles])
    halo_s = pair(5, to_right.at[0], from_left.at[0], to_left.at[0], from_right.at[0])
    early = place != 1
    pl.when(early)(lambda: tell(halo_h))
    for j in range(4):
        f2[j] = raw_f[4 * j + 2].T
        f3[j] = raw_f[4 * j + 3].T

    @pl.when(place == 0)
    def _():
        hold[0, pl.ds(8, C), :] = raw_u[...].T

    @pl.when(place > 0)
    def _():
        prev_copy.wait_recv()
        hold[0, pl.ds(8, C), :] = prev[...].T

    to_right[0, pl.ds(0, 6), :] = hold[0, pl.ds(8 + C - 6, 6), :]
    to_left[0, pl.ds(0, 6), :] = hold[0, pl.ds(8, 6), :]
    pl.when(early)(lambda: tell(halo_s))

    def differences(lo, n):
        x, y, diffusion = (kraw[i, pl.ds(lo - Z, n), :] for i in range(3))
        row = lax.broadcasted_iota(jnp.int32, (n, C), 1)
        west = jnp.maximum(x, 0.0) + diffusion
        east = diffusion - jnp.minimum(x, 0.0)
        south = jnp.maximum(y, 0.0) + diffusion
        north = diffusion - jnp.minimum(y, 0.0)
        rows = pl.ds(lo, n)
        base[0, rows, :] = jnp.where(row == 0, 0.0, west)
        base[1, rows, :] = jnp.where(row == C - 1, 0.0, east)
        base[2, rows, :] = south
        base[3, rows, :] = north
        base[4, rows, :] = (west + east) + (south + north)

    first = Z + H
    main = pl.ds(first, C)
    span = pl.ds(Z, W)
    fields = [(i,) for i in range(4)]
    differences(first, C)
    for j in range(4):
        build(base, coef, first + 32 * j, 32)

    def source(level, i, col, n):
        if level < 2:
            return hold[4 + 4 * level + i, pl.ds(8 + col, n), :]
        if level == 2:
            return f2[i, pl.ds(col, n), :]
        at_end = hold[1 + i, pl.ds(8 + col, n), :] if i < 3 else g3[pl.ds(col, n), :]
        return f3[i, pl.ds(col, n), :] - at_end

    levels = (sa, sb, sc, sd, rp)
    for i in range(4):
        sa[i, main, :] = hold[i, pl.ds(8, C), :]
    for level in range(4):
        for col in (0, 64):
            for (i,) in fields:
                levels[level + 1][i, pl.ds(first + col, 64), :] = (
                    heun(coef, 0, levels[level], (i,), first + col, 64) + source(level, i, col, 64))

    def single(m, src, at, dst, term, parts):
        for lo, n in parts:
            dst[pl.ds(lo, n), :] = heun(coef, m, src, at, lo, n) + term(lo, n)

    def rows_of(ref, *at):
        return lambda lo, n: ref[at + (pl.ds(lo, n),)]

    def right_side(parts):
        single(1, rp, (0,), la, rows_of(rp, 1), parts)
        single(1, la, (), lb, rows_of(rp, 2), parts)
        single(1, lb, (), y2, rows_of(rp, 3), parts)

    inner = [(first + 32 * j, 32) for j in range(4)]
    whole = [(Z + 32 * j, 32) for j in range(5)]
    right_side(inner)

    arrive(*halo_k[0][:2])

    @pl.when(place == 1)
    def _():
        tell(halo_h)
        tell(halo_s)

    differences(Z, H)
    differences(first + C, H)
    build(base, coef, Z, 24)
    build(base, coef, first + C - 8, 24)
    for level in range(4):
        for (i,) in fields:
            x = heun(coef, 0, levels[level], (i,), first - 8, 16)
            levels[level + 1][i, pl.ds(first - 8, 8), :] = x[:8]
            levels[level + 1][i, pl.ds(first, 8), :] = x[8:] + source(level, i, 0, 8)
            x = heun(coef, 0, levels[level], (i,), first + C - 8, 16)
            levels[level + 1][i, pl.ds(first + C - 8, 8), :] = x[:8] + source(level, i, C - 8, 8)
            levels[level + 1][i, pl.ds(first + C, 8), :] = x[8:]

    halo_r = both(7, rp.at[0, pl.ds(Z + C, 24), :], rsl.at[0], rp.at[0, pl.ds(Z + H - 8, 24), :], rsr.at[0])
    halo_t = both(20, rp.at[pl.ds(1, 2), pl.ds(Z + C + 8, 16), :], rsl.at[pl.ds(1, 2), pl.ds(8, 16), :],
                  rp.at[pl.ds(1, 2), pl.ds(Z + H - 8, 16), :], rsr.at[pl.ds(1, 2), pl.ds(0, 16), :])

    right_side([(Z, 2 * H), (Z + C, 2 * H)])

    hand = copy_of(9, y2.at[span, :], y1p.at[span, :], tm, 1, c)

    @pl.when(sx == 0)
    def _():
        hand.start()
        y1[...] = y2[span, :]

    @pl.when(sx == 1)
    def _():
        hand.wait_recv()
        y1[...] = y1p[span, :]

    cross_main = copy_of(14, e1p.at[span, :], em, 1, 1, c)
    relay = copy_of(15, em, em, 1, 0, c, at=14)
    cross_sides = []
    for s in (1, 0):
        cross_sides.append((copy_of(16 + s, e1p.at[pl.ds(Z + C, 2 * H), :], el, 1, s, right, at=16),
                            copy_of(18 + s, e1p.at[pl.ds(Z, 2 * H), :], er, 1, s, left, at=17)))

    @pl.when(place == 1)
    def _():
        single(2, y1p, (), e1p, rows_of(y2), whole)
        cross_main.start()
        for up, down in cross_sides:
            pl.when(has_right)(up.start)
            pl.when(has_left)(down.start)
        yl[...] = e1p[span, :]

    @pl.when(place != 1)
    def _():
        yl[...] = y2[span, :]

    edge_1 = both(10, y1.at[pl.ds(C, 2 * H), :], rl, y1.at[pl.ds(0, 2 * H), :], rr)
    edge_2 = pair(12, yl.at[pl.ds(H + C, H), :], rl2, yl.at[pl.ds(0, H), :], rr2)
    pl.when(sx == 1)(lambda: tell(edge_2))

    def joined(dst, own, from_left, from_right, middle=True):
        dst[pl.ds(Z, 2 * H), :] = own[pl.ds(0, 2 * H), :] + from_left[...]
        dst[pl.ds(Z + C, 2 * H), :] = own[pl.ds(C, 2 * H), :] + from_right[...]
        if middle:
            dst[pl.ds(Z + 2 * H, C - 2 * H), :] = own[pl.ds(2 * H, C - 2 * H), :]

    y1f[pl.ds(Z + 2 * H, C - 2 * H), :] = y1[pl.ds(2 * H, C - 2 * H), :]
    y2f[pl.ds(H, C - 2 * H), :] = yl[pl.ds(2 * H, C - 2 * H), :]
    for i in range(3):
        rf[i, pl.ds(Z + 24, W - 48), :] = rp[i, pl.ds(Z + 24, W - 48), :]

    def sums():
        y2f[pl.ds(0, H), :] = yl[pl.ds(H, H), :] + rl2[...]
        y2f[pl.ds(C - H, H), :] = yl[pl.ds(C, H), :] + rr2[...]
        joined(y1f, y1, rl, rr, False)
        for i in range(3):
            if i == 0:
                rf[i, pl.ds(Z, 24), :] = rp[i, pl.ds(Z, 24), :] + rsl[i]
                rf[i, pl.ds(Z + W - 24, 24), :] = rp[i, pl.ds(Z + W - 24, 24), :] + rsr[i]
            else:
                rf[i, pl.ds(Z + 8, 16), :] = rp[i, pl.ds(Z + 8, 16), :] + rsl[i, pl.ds(8, 16), :]
                rf[i, pl.ds(Z + W - 24, 16), :] = rp[i, pl.ds(Z + W - 24, 16), :] + rsr[i, pl.ds(0, 16), :]

    later = tm == 1
    pl.when(later)(cross_main.wait_recv)
    pl.when(place == 3)(relay.start)

    @pl.when(place == 1)
    def _():
        bf[span, :] = y1p[span, :]

    @pl.when(place == 2)
    def _():
        bf[span, :] = em[...]

    @pl.when(place == 3)
    def _():
        e1[span, :] = em[...]
        single(2, e1, (), bf, rows_of(y1p), whole)

    chain = ((bf, la), (la, lb), (lb, lc))
    starts = (bf, la, lb, lc)

    for i, (src, dst) in enumerate(chain):
        single(1, src, (), dst, rows_of(rp, i), inner)
    for (i,) in fields:
        sa[i, main, :] = hold[i, pl.ds(8, C), :] + starts[i][main, :]
    for level in range(3):
        for col in (0, 64):
            for (i,) in fields:
                levels[level + 1][i, pl.ds(first + col, 64), :] = (
                    heun(coef, 0, levels[level], (i,), first + col, 64) + source(level, i, col, 64))

    for copies in (edge_1, halo_r, halo_t, halo_h, halo_s):
        arrive(*copies)
    pl.when(sx == 1)(lambda: arrive(*edge_2))

    @pl.when((sx == 0) | (c == 0))
    def _():
        rl2[...] = jnp.zeros_like(rl2)

    @pl.when((sx == 0) | (c == count - 1))
    def _():
        rr2[...] = jnp.zeros_like(rr2)

    sums()
    for i in range(4):
        hold[i, pl.ds(2, 6), :] = from_left[i, pl.ds(0, 6), :]
        hold[i, pl.ds(8 + C, 6), :] = from_right[i, pl.ds(0, 6), :]
        hold[4 + i, pl.ds(4, 4), :] = from_left[4 + i // 2, pl.ds(4 * (i % 2), 4), :]
        hold[4 + i, pl.ds(8 + C, 4), :] = from_right[4 + i // 2, pl.ds(4 * (i % 2), 4), :]
        hold[8 + i, pl.ds(6, 2), :] = from_left[i, pl.ds(6, 2), :]
        hold[8 + i, pl.ds(8 + C, 2), :] = from_right[i, pl.ds(6, 2), :]
    pl.when(later & has_left)(cross_sides[0][0].wait_recv)
    pl.when(later & has_right)(cross_sides[0][1].wait_recv)

    @pl.when(place == 1)
    def _():
        bf[span, :] = y1f[span, :]

    @pl.when(place == 2)
    def _():
        joined(bf, em, el, er)

    edges = [(Z, 48), (Z + W - 48, 48)]

    @pl.when(place == 3)
    def _():
        joined(e1, em, el, er)
        single(2, e1, (), bf, rows_of(y1f), edges)

    def correct(i):
        src, dst = chain[i]
        single(1, src, (), dst, rows_of(rf, i), edges)

    def begin(i):
        for lo in (first - 8, first + C - 32):
            sa[i, pl.ds(lo, 40), :] = hold[i, pl.ds(lo - first + 8, 40), :] + starts[i][pl.ds(lo, 40), :]
        if i:
            out[4 * i - 1] = sa[i, main, :].T

    def relax(i, level):
        for lo, n in ((first - 8, 40), (first + C - 32, 40)) if level < 2 else ((first, 32), (first + C - 32, 32)):
            levels[level + 1][i, pl.ds(lo, n), :] = (
                heun(coef, 0, levels[level], (i,), lo, n) + source(level, i, lo - first, n))
        out[4 * i + level] = levels[level + 1][i, main, :].T

    begin(0)
    correct(0)
    relax(0, 0)
    begin(1)
    correct(1)
    relax(0, 1)
    relax(1, 0)
    begin(2)
    correct(2)
    relax(0, 2)
    relax(1, 1)
    relax(2, 0)
    begin(3)
    right_after = jnp.where(sx == 0, y1f[main, :], y2f[...])
    own = jnp.concatenate([heun(coef, 2, bf, (), lo, n) for lo, n in inner], 0)
    out[15] = (g3[...] + (right_after + jnp.where(place == 1, 0.0, own))).T
    relax(1, 2)
    relax(2, 1)
    relax(3, 0)
    relax(2, 2)
    relax(3, 1)
    relax(3, 2)

    for up, down in sent:
        told = sx == 1 if up is edge_2[0] else True
        pl.when(told & has_right)(up.wait_send)
        pl.when(told & has_left)(down.wait_send)
    for up, down, told in halo_k:
        pl.when(told & has_right)(up.wait_send)
        pl.when(told & has_left)(down.wait_send)

    @pl.when(place < 3)
    def _():
        prev_copy.wait_send()

    @pl.when(sx == 0)
    def _():
        hand.wait_send()

    @pl.when(place == 1)
    def _():
        cross_main.wait_send()
        for up, down in cross_sides:
            pl.when(has_right)(up.wait_send)
            pl.when(has_left)(down.wait_send)

    pl.when(place == 3)(relay.wait_send)


def local(u_init, guess, forcing, speed_x, speed_y, diffusion):
    def vmem(*shape):
        return pltpu.VMEM(shape, F32)

    any_space = pl.BlockSpec(memory_space=pltpu.HBM)
    field = (N, C)
    return pl.pallas_call(
        kernel,
        out_shape=pltpu.VMEM(forcing.shape, F32),
        in_specs=[any_space] * 6,
        out_specs=pl.BlockSpec(memory_space=pltpu.VMEM),
        scratch_shapes=[
            vmem(3, C, C), vmem(C, C), vmem(4, C, C), vmem(16, C, C), vmem(C, C),
            vmem(3, W, C), vmem(5, *field), vmem(3, 13, W, C),
            vmem(12, C + 16, C), vmem(C, C), vmem(4, C, C), vmem(4, C, C),
            *(vmem(4, *field) for _ in range(5)), vmem(3, *field),
            vmem(*field), vmem(*field), vmem(*field),
            vmem(*field), vmem(W, C), vmem(*field), vmem(*field), vmem(C, C),
            vmem(*field), vmem(*field), vmem(*field),
            vmem(W, C), vmem(2 * H, C), vmem(2 * H, C),
            vmem(2 * H, C), vmem(2 * H, C), vmem(H, C), vmem(H, C), vmem(W, C),
            vmem(3, 24, C), vmem(3, 24, C), *(vmem(6, 8, C) for _ in range(4)),
            pltpu.SemaphoreType.DMA((6,)),
            pltpu.SemaphoreType.DMA((22,)),
            pltpu.SemaphoreType.DMA((22,)),
            pltpu.SemaphoreType.DMA((4,)),
        ],
        compiler_params=pltpu.CompilerParams(collective_id=0, has_side_effects=True, vmem_limit_bytes=60 << 20),
    )(u_init, guess, forcing, speed_x, speed_y, diffusion)


def solution(mesh):
    placed = (
        P(None, "sy"),
        P(("tm", "sx"), None, "sy"),
        P(("tm", "sx"), None, "sy"),
        P(None, "sy"),
        P(None, "sy"),
        P(None, "sy"),
    )
    return jax.shard_map(
        local, mesh=mesh, in_specs=placed, out_specs=P(("tm", "sx"), None, "sy"), check_vma=False
    )
```

time: 20.6 us -> 19.2 us (0.932)
  the two profiles are of different devices: /device:TPU:161 before, /device:TPU:165 now
where the time goes in v4:
time: 19.2 us; the launch traced here: 19.1 us
  Pallas kernels  18.1 us (94%)
  local copies, waits for them, and re-layouts  0.97 us (5%)
    pallas_call x1, Pallas kernels, local(): pl.pallas_call(kernel, out_shape=pltpu.VMEM(forcing.shape, F32), in_specs...  18.1 us
    unnamed x1, local copies, waits for them, and re-layouts  0.97 us

profile of v4, /device:TPU:165, one launch (start us, length us, event | category | flops | bytes accessed | tf_op | source)
XLA Modules:
  0.0 19.1 jit_solution(5295506898075044667)
XLA Ops:
  0.0 18.1 %shard_map.64 = f32[16,128,128]{2,1,0:T(8,128)S(1)} custom-call(f32[128,128]{1,0:T(8,128)} %u_hbm.1, f32[4,128,128]{2,1,0:T(8,128)} %guess_hbm.1, f32[16,128,128]{2,1,0:T(8,128)} %forcing_hbm.1, f32[128,128]{1,0:T(8,128)} %sx_hbm.1, f32[128,128]{1,0:T(8,128)} %sy_hbm.1, f32[128,128]{1,0:T(8,128)} %d_hbm.1), custom_call_target="tpu_custom_call" | custom-call | tf_op jit(solution)/shard_map/pallas_call | solution.py:506
  18.1 1.0 %copy.8 = f32[16,128,128]{2,1,0:T(8,128)} copy(f32[16,128,128]{2,1,0:T(8,128)S(1)} %shard_map.64) | data formatting | bytes 2097152

commit v5 on v4

--- a/solution.py
+++ b/solution.py
@@ -71,8 +71,8 @@
 
 def kernel(u_hbm, guess_hbm, forcing_hbm, sx_hbm, sy_hbm, d_hbm, out,
            raw_k, raw_u, raw_g, raw_f, prev, kraw, base, coef, hold, g3, f2, f3, sa, sb, sc, sd, rp, rf,
-           la, lb, lc, y1p, y1, y2, y1f, y2f, e1p, e1, bf, em, el, er, rl, rr, rl2, rr2, yl, rsl, rsr, to_left, to_right, from_left, from_right,
-           lsem, ssem, rsem, k_sem):
+           la, lb, lc, y1p, y1, y2, y1f, y2f, e1p, e1, bf, handed, em, em_low, em_high, el, er, rl, rr, rl2, rr2, yl, rsl, rsr, to_left, to_right, from_left, from_right,
+           lsem, ssem, rsem, k_sem, e_sem):
     tm, sx, c = lax.axis_index("tm"), lax.axis_index("sx"), lax.axis_index("sy")
     count = lax.axis_size("sy")
     place = 2 * tm + sx
@@ -110,7 +110,7 @@
         greet(0, 0, c)
         greet(0, 1, c)
 
-    for ref in (sa, sb, sc, sd, rp, rf, la, lb, lc, bf, base):
+    for ref in (sa, sb, sc, sd, rp, rf, la, lb, lc, bf, base, e1p):
         ref[...] = jnp.zeros_like(ref)
     for ref in (y1p, y1f, y2, e1p, e1):
         ref[pl.ds(0, Z), :] = jnp.zeros((Z, ref.shape[1]), F32)
@@ -211,19 +211,6 @@
         f2[j] = raw_f[4 * j + 2].T
         f3[j] = raw_f[4 * j + 3].T
 
-    @pl.when(place == 0)
-    def _():
-        hold[0, pl.ds(8, C), :] = raw_u[...].T
-
-    @pl.when(place > 0)
-    def _():
-        prev_copy.wait_recv()
-        hold[0, pl.ds(8, C), :] = prev[...].T
-
-    to_right[0, pl.ds(0, 6), :] = hold[0, pl.ds(8 + C - 6, 6), :]
-    to_left[0, pl.ds(0, 6), :] = hold[0, pl.ds(8, 6), :]
-    pl.when(early)(lambda: tell(halo_s))
-
     def differences(lo, n):
         x, y, diffusion = (kraw[i, pl.ds(lo - Z, n), :] for i in range(3))
         row = lax.broadcasted_iota(jnp.int32, (n, C), 1)
@@ -255,13 +242,31 @@
         return f3[i, pl.ds(col, n), :] - at_end
 
     levels = (sa, sb, sc, sd, rp)
-    for i in range(4):
-        sa[i, main, :] = hold[i, pl.ds(8, C), :]
-    for level in range(4):
-        for col in (0, 64):
-            for (i,) in fields:
-                levels[level + 1][i, pl.ds(first + col, 64), :] = (
-                    heun(coef, 0, levels[level], (i,), first + col, 64) + source(level, i, col, 64))
+    def relax_inner(which):
+        for i in which:
+            sa[i, main, :] = hold[i, pl.ds(8, C), :]
+        for level in range(4):
+            for col in (0, 64):
+                for i in which:
+                    levels[level + 1][i, pl.ds(first + col, 64), :] = (
+                        heun(coef, 0, levels[level], (i,), first + col, 64) + source(level, i, col, 64))
+
+    relax_inner((1, 2, 3))
+
+    @pl.when(place == 0)
+    def _():
+        hold[0, pl.ds(8, C), :] = raw_u[...].T
+
+    @pl.when(place > 0)
+    def _():
+        prev_copy.wait_recv()
+        hold[0, pl.ds(8, C), :] = prev[...].T
+
+    to_right[0, pl.ds(0, 6), :] = hold[0, pl.ds(8 + C - 6, 6), :]
+    to_left[0, pl.ds(0, 6), :] = hold[0, pl.ds(8, 6), :]
+    pl.when(early)(lambda: tell(halo_s))
+
+    relax_inner((0,))
 
     def single(m, src, at, dst, term, parts):
         for lo, n in parts:
@@ -278,6 +283,28 @@
     inner = [(first + 32 * j, 32) for j in range(4)]
     whole = [(Z + 32 * j, 32) for j in range(5)]
     right_side(inner)
+
+    core = pl.ds(first + 16, C - 32)
+    sides_of = (pl.ds(Z, 2 * H), pl.ds(Z + C, 2 * H))
+    hand_in = copy_of(9, y2.at[core, :], y1p.at[core, :], tm, 1, c)
+    hand_out = [copy_of(22 + i, y2.at[rows, :], handed.at[i], tm, 1, c) for i, rows in enumerate(sides_of)]
+    cross_in = copy_of(14, e1p.at[core, :], em, 1, 1, c)
+    relay = copy_of(15, em, em, 1, 0, c, at=14)
+    low, high = pl.ds(Z, 40), pl.ds(Z + W - 40, 40)
+    cross_out, cross_sides = [], []
+    for s in (1, 0):
+        cross_sides.append((copy_of(16 + s, e1p.at[pl.ds(Z + C, 2 * H), :], el, 1, s, right, at=16),
+                            copy_of(18 + s, e1p.at[pl.ds(Z, 2 * H), :], er, 1, s, left, at=17)))
+        cross_out.append((copy_of(24 + s, e1p.at[low, :], em_low, 1, s, c, at=24),
+                          copy_of(26 + s, e1p.at[high, :], em_high, 1, s, c, at=25)))
+
+    pl.when(sx == 0)(hand_in.start)
+    pl.when(place == 1)(hand_in.wait_recv)
+
+    @pl.when(place == 1)
+    def _():
+        single(2, y1p, (), e1p, rows_of(y2), [(first + 16, 48), (first + 64, 48)])
+        cross_in.start()
 
     arrive(*halo_k[0][:2])
 
@@ -305,30 +332,35 @@
 
     right_side([(Z, 2 * H), (Z + C, 2 * H)])
 
-    hand = copy_of(9, y2.at[span, :], y1p.at[span, :], tm, 1, c)
+
+    edge_1 = []
+    for to in range(2):
+        edge_1.append((make_copy(y2.at[pl.ds(Z + C, 2 * H), :], rl, e_sem.at[2 * to], rsem.at[10], tm, to, right),
+                       make_copy(y2.at[pl.ds(Z, 2 * H), :], rr, e_sem.at[2 * to + 1], rsem.at[11], tm, to, left)))
 
     @pl.when(sx == 0)
     def _():
-        hand.start()
+        for copy in hand_out:
+            copy.start()
+        for to in (1, 0):
+            tell(edge_1[to])
         y1[...] = y2[span, :]
 
     @pl.when(sx == 1)
     def _():
-        hand.wait_recv()
+        pl.when(tm == 1)(hand_in.wait_recv)
+        for i, copy in enumerate(hand_out):
+            copy.wait_recv()
+            y1p[sides_of[i], :] = handed[i]
         y1[...] = y1p[span, :]
 
-    cross_main = copy_of(14, e1p.at[span, :], em, 1, 1, c)
-    relay = copy_of(15, em, em, 1, 0, c, at=14)
-    cross_sides = []
-    for s in (1, 0):
-        cross_sides.append((copy_of(16 + s, e1p.at[pl.ds(Z + C, 2 * H), :], el, 1, s, right, at=16),
-                            copy_of(18 + s, e1p.at[pl.ds(Z, 2 * H), :], er, 1, s, left, at=17)))
-
     @pl.when(place == 1)
     def _():
-        single(2, y1p, (), e1p, rows_of(y2), whole)
-        cross_main.start()
-        for up, down in cross_sides:
+        cross_in.wait_send()
+        single(2, y1p, (), e1p, rows_of(y2), [(Z, 40), (Z + W - 40, 40)])
+        for (up, down), outer in zip(cross_sides, cross_out):
+            for copy in outer:
+                copy.start()
             pl.when(has_right)(up.start)
             pl.when(has_left)(down.start)
         yl[...] = e1p[span, :]
@@ -337,7 +369,6 @@
     def _():
         yl[...] = y2[span, :]
 
-    edge_1 = both(10, y1.at[pl.ds(C, 2 * H), :], rl, y1.at[pl.ds(0, 2 * H), :], rr)
     edge_2 = pair(12, yl.at[pl.ds(H + C, H), :], rl2, yl.at[pl.ds(0, H), :], rr2)
     pl.when(sx == 1)(lambda: tell(edge_2))
 
@@ -353,8 +384,6 @@
         rf[i, pl.ds(Z + 24, W - 48), :] = rp[i, pl.ds(Z + 24, W - 48), :]
 
     def sums():
-        y2f[pl.ds(0, H), :] = yl[pl.ds(H, H), :] + rl2[...]
-        y2f[pl.ds(C - H, H), :] = yl[pl.ds(C, H), :] + rr2[...]
         joined(y1f, y1, rl, rr, False)
         for i in range(3):
             if i == 0:
@@ -365,7 +394,7 @@
                 rf[i, pl.ds(Z + W - 24, 16), :] = rp[i, pl.ds(Z + W - 24, 16), :] + rsr[i, pl.ds(0, 16), :]
 
     later = tm == 1
-    pl.when(later)(cross_main.wait_recv)
+    pl.when(later)(cross_in.wait_recv)
     pl.when(place == 3)(relay.start)
 
     @pl.when(place == 1)
@@ -374,12 +403,12 @@
 
     @pl.when(place == 2)
     def _():
-        bf[span, :] = em[...]
+        bf[core, :] = em[...]
 
     @pl.when(place == 3)
     def _():
-        e1[span, :] = em[...]
-        single(2, e1, (), bf, rows_of(y1p), whole)
+        e1[core, :] = em[...]
+        single(2, e1, (), bf, rows_of(y1p), inner)
 
     chain = ((bf, la), (la, lb), (lb, lc))
     starts = (bf, la, lb, lc)
@@ -394,18 +423,8 @@
                 levels[level + 1][i, pl.ds(first + col, 64), :] = (
                     heun(coef, 0, levels[level], (i,), first + col, 64) + source(level, i, col, 64))
 
-    for copies in (edge_1, halo_r, halo_t, halo_h, halo_s):
+    for copies in (edge_1[0], halo_r, halo_t, halo_h, halo_s):
         arrive(*copies)
-    pl.when(sx == 1)(lambda: arrive(*edge_2))
-
-    @pl.when((sx == 0) | (c == 0))
-    def _():
-        rl2[...] = jnp.zeros_like(rl2)
-
-    @pl.when((sx == 0) | (c == count - 1))
-    def _():
-        rr2[...] = jnp.zeros_like(rr2)
-
     sums()
     for i in range(4):
         hold[i, pl.ds(2, 6), :] = from_left[i, pl.ds(0, 6), :]
@@ -414,22 +433,34 @@
         hold[4 + i, pl.ds(8 + C, 4), :] = from_right[4 + i // 2, pl.ds(4 * (i % 2), 4), :]
         hold[8 + i, pl.ds(6, 2), :] = from_left[i, pl.ds(6, 2), :]
         hold[8 + i, pl.ds(8 + C, 2), :] = from_right[i, pl.ds(6, 2), :]
+    @pl.when(later)
+    def _():
+        for copy in cross_out[0]:
+            copy.wait_recv()
+
     pl.when(later & has_left)(cross_sides[0][0].wait_recv)
     pl.when(later & has_right)(cross_sides[0][1].wait_recv)
 
+    edges = [(Z, 48), (Z + W - 48, 48)]
+
+    def crossed(dst):
+        dst[pl.ds(Z, 2 * H), :] = em_low[pl.ds(0, 2 * H), :] + el[...]
+        dst[pl.ds(Z + 2 * H, 8), :] = em_low[pl.ds(2 * H, 8), :]
+        dst[pl.ds(Z + C - 8, 8), :] = em_high[pl.ds(0, 8), :]
+        dst[pl.ds(Z + C, 2 * H), :] = em_high[pl.ds(8, 2 * H), :] + er[...]
+
     @pl.when(place == 1)
     def _():
         bf[span, :] = y1f[span, :]
 
     @pl.when(place == 2)
     def _():
-        joined(bf, em, el, er)
-
-    edges = [(Z, 48), (Z + W - 48, 48)]
+        crossed(bf)
+
 
     @pl.when(place == 3)
     def _():
-        joined(e1, em, el, er)
+        crossed(e1)
         single(2, e1, (), bf, rows_of(y1f), edges)
 
     def correct(i):
@@ -461,21 +492,33 @@
     relax(1, 1)
     relax(2, 0)
     begin(3)
-    right_after = jnp.where(sx == 0, y1f[main, :], y2f[...])
-    own = jnp.concatenate([heun(coef, 2, bf, (), lo, n) for lo, n in inner], 0)
-    out[15] = (g3[...] + (right_after + jnp.where(place == 1, 0.0, own))).T
     relax(1, 2)
     relax(2, 1)
     relax(3, 0)
     relax(2, 2)
     relax(3, 1)
     relax(3, 2)
+    pl.when(sx == 1)(lambda: arrive(*edge_2))
+
+    @pl.when((sx == 0) | (c == 0))
+    def _():
+        rl2[...] = jnp.zeros_like(rl2)
+
+    @pl.when((sx == 0) | (c == count - 1))
+    def _():
+        rr2[...] = jnp.zeros_like(rr2)
+
+    y2f[pl.ds(0, H), :] = yl[pl.ds(H, H), :] + rl2[...]
+    y2f[pl.ds(C - H, H), :] = yl[pl.ds(C, H), :] + rr2[...]
+    right_after = jnp.where(sx == 0, y1f[main, :], y2f[...])
+    own = jnp.concatenate([heun(coef, 2, bf, (), lo, n) for lo, n in inner], 0)
+    out[15] = (g3[...] + (right_after + jnp.where(place == 1, 0.0, own))).T
 
     for up, down in sent:
         told = sx == 1 if up is edge_2[0] else True
         pl.when(told & has_right)(up.wait_send)
         pl.when(told & has_left)(down.wait_send)
-    for up, down, told in halo_k:
+    for up, down, told in halo_k + [copies + (sx == 0,) for copies in edge_1]:
         pl.when(told & has_right)(up.wait_send)
         pl.when(told & has_left)(down.wait_send)
 
@@ -485,11 +528,14 @@
 
     @pl.when(sx == 0)
     def _():
-        hand.wait_send()
+        hand_in.wait_send()
+        for copy in hand_out:
+            copy.wait_send()
 
     @pl.when(place == 1)
     def _():
-        cross_main.wait_send()
+        for copy in cross_out[0] + cross_out[1]:
+            copy.wait_send()
         for up, down in cross_sides:
             pl.when(has_right)(up.wait_send)
             pl.when(has_left)(down.wait_send)
@@ -516,12 +562,13 @@
             vmem(*field), vmem(*field), vmem(*field),
             vmem(*field), vmem(W, C), vmem(*field), vmem(*field), vmem(C, C),
             vmem(*field), vmem(*field), vmem(*field),
-            vmem(W, C), vmem(2 * H, C), vmem(2 * H, C),
+            vmem(2, 2 * H, C), vmem(C - 32, C), vmem(40, C), vmem(40, C), vmem(2 * H, C), vmem(2 * H, C),
             vmem(2 * H, C), vmem(2 * H, C), vmem(H, C), vmem(H, C), vmem(W, C),
             vmem(3, 24, C), vmem(3, 24, C), *(vmem(6, 8, C) for _ in range(4)),
             pltpu.SemaphoreType.DMA((6,)),
-            pltpu.SemaphoreType.DMA((22,)),
-            pltpu.SemaphoreType.DMA((22,)),
+            pltpu.SemaphoreType.DMA((28,)),
+            pltpu.SemaphoreType.DMA((28,)),
+            pltpu.SemaphoreType.DMA((4,)),
             pltpu.SemaphoreType.DMA((4,)),
         ],
         compiler_params=pltpu.CompilerParams(collective_id=0, has_side_effects=True, vmem_limit_bytes=60 << 20),

time: 19.2 us -> 17.9 us (0.932)
  the two profiles are of different devices: /device:TPU:165 before, /device:TPU:132 now
where the time goes in v5:
time: 17.9 us; the launch traced here: 17.8 us
  Pallas kernels  16.8 us (94%)
  local copies, waits for them, and re-layouts  0.97 us (5%)
    pallas_call x1, Pallas kernels, local(): pl.pallas_call(kernel, out_shape=pltpu.VMEM(forcing.shape, F32), in_specs...  16.8 us
    unnamed x1, local copies, waits for them, and re-layouts  0.97 us

profile of v5, /device:TPU:132, one launch (start us, length us, event | category | flops | bytes accessed | tf_op | source)
XLA Modules:
  0.0 17.8 jit_solution(1664997377587386542)
XLA Ops:
  0.0 16.8 %shard_map.64 = f32[16,128,128]{2,1,0:T(8,128)S(1)} custom-call(f32[128,128]{1,0:T(8,128)} %u_hbm.1, f32[4,128,128]{2,1,0:T(8,128)} %guess_hbm.1, f32[16,128,128]{2,1,0:T(8,128)} %forcing_hbm.1, f32[128,128]{1,0:T(8,128)} %sx_hbm.1, f32[128,128]{1,0:T(8,128)} %sy_hbm.1, f32[128,128]{1,0:T(8,128)} %d_hbm.1), custom_call_target="tpu_custom_call" | custom-call | tf_op jit(solution)/shard_map/pallas_call | solution.py:552
  16.8 1.0 %copy.8 = f32[16,128,128]{2,1,0:T(8,128)} copy(f32[16,128,128]{2,1,0:T(8,128)S(1)} %shard_map.64) | data formatting | bytes 2097152

commit v6 on v5

--- a/solution.py
+++ b/solution.py
@@ -340,10 +340,10 @@
 
     @pl.when(sx == 0)
     def _():
+        for to in (1, 0):
+            tell(edge_1[to])
         for copy in hand_out:
             copy.start()
-        for to in (1, 0):
-            tell(edge_1[to])
         y1[...] = y2[span, :]
 
     @pl.when(sx == 1)
@@ -471,13 +471,13 @@
         for lo in (first - 8, first + C - 32):
             sa[i, pl.ds(lo, 40), :] = hold[i, pl.ds(lo - first + 8, 40), :] + starts[i][pl.ds(lo, 40), :]
         if i:
-            out[4 * i - 1] = sa[i, main, :].T
+            out[4 * i - 1] = sa[i, main, :]
 
     def relax(i, level):
         for lo, n in ((first - 8, 40), (first + C - 32, 40)) if level < 2 else ((first, 32), (first + C - 32, 32)):
             levels[level + 1][i, pl.ds(lo, n), :] = (
                 heun(coef, 0, levels[level], (i,), lo, n) + source(level, i, lo - first, n))
-        out[4 * i + level] = levels[level + 1][i, main, :].T
+        out[4 * i + level] = levels[level + 1][i, main, :]
 
     begin(0)
     correct(0)
@@ -512,7 +512,7 @@
     y2f[pl.ds(C - H, H), :] = yl[pl.ds(C, H), :] + rr2[...]
     right_after = jnp.where(sx == 0, y1f[main, :], y2f[...])
     own = jnp.concatenate([heun(coef, 2, bf, (), lo, n) for lo, n in inner], 0)
-    out[15] = (g3[...] + (right_after + jnp.where(place == 1, 0.0, own))).T
+    out[15] = g3[...] + (right_after + jnp.where(place == 1, 0.0, own))
 
     for up, down in sent:
         told = sx == 1 if up is edge_2[0] else True
@@ -549,7 +549,7 @@
 
     any_space = pl.BlockSpec(memory_space=pltpu.HBM)
     field = (N, C)
-    return pl.pallas_call(
+    by_column = pl.pallas_call(
         kernel,
         out_shape=pltpu.VMEM(forcing.shape, F32),
         in_specs=[any_space] * 6,
@@ -573,6 +573,7 @@
         ],
         compiler_params=pltpu.CompilerParams(collective_id=0, has_side_effects=True, vmem_limit_bytes=60 << 20),
     )(u_init, guess, forcing, speed_x, speed_y, diffusion)
+    return jnp.swapaxes(by_column, 1, 2)
 
 
 def solution(mesh):

time: 17.9 us -> 17.7 us (0.989)
  Pallas kernels: 16.8 us -> 16.3 us
  local copies, waits for them, and re-layouts: 0.97 us -> 1.31 us
    transpose x0 -> x1, local copies, waits for them, and re-layouts: none -> 1.31 us  [local(): return jnp.swapaxes(by_column, 1, 2)]
    unnamed x1 -> x0, local copies, waits for them, and re-layouts: 0.97 us -> none
    pallas_call x1, Pallas kernels: 16.8 us -> 16.3 us  [local(): pl.pallas_call(kernel, out_shape=pltpu.VMEM(forcing.shape, F32), in_specs...]
where the time goes in v6:
time: 17.7 us; the launch traced here: 17.6 us
  Pallas kernels  16.3 us (92%)
  local copies, waits for them, and re-layouts  1.31 us (7%)
    pallas_call x1, Pallas kernels, local(): pl.pallas_call(kernel, out_shape=pltpu.VMEM(forcing.shape, F32), in_specs...  16.3 us
    transpose x1, local copies, waits for them, and re-layouts, local(): return jnp.swapaxes(by_column, 1, 2)  1.31 us

profile of v6, /device:TPU:132, one launch (start us, length us, event | category | flops | bytes accessed | tf_op | source)
XLA Modules:
  0.0 17.6 jit_solution(5703096699296364067)
XLA Ops:
  0.0 16.3 %shard_map.64 = f32[16,128,128]{2,1,0:T(8,128)S(1)} custom-call(f32[128,128]{1,0:T(8,128)} %u_hbm.1, f32[4,128,128]{2,1,0:T(8,128)} %guess_hbm.1, f32[16,128,128]{2,1,0:T(8,128)} %forcing_hbm.1, f32[128,128]{1,0:T(8,128)} %sx_hbm.1, f32[128,128]{1,0:T(8,128)} %sy_hbm.1, f32[128,128]{1,0:T(8,128)} %d_hbm.1), custom_call_target="tpu_custom_call" | custom-call | tf_op jit(solution)/shard_map/pallas_call | solution.py:552
  16.3 1.3 %copy.7 = f32[16,128,128]{2,1,0:T(8,128)} copy(f32[16,128,128]{1,2,0:T(8,128)S(1)} %bitcast.1) | data formatting | bytes 2097152 | tf_op jit(solution)/shard_map/transpose | solution.py:576

commit v7 on v6

--- a/solution.py
+++ b/solution.py
@@ -423,9 +423,8 @@
                 levels[level + 1][i, pl.ds(first + col, 64), :] = (
                     heun(coef, 0, levels[level], (i,), first + col, 64) + source(level, i, col, 64))
 
-    for copies in (edge_1[0], halo_r, halo_t, halo_h, halo_s):
-        arrive(*copies)
-    sums()
+    arrive(*halo_h)
+    arrive(*halo_s)
     for i in range(4):
         hold[i, pl.ds(2, 6), :] = from_left[i, pl.ds(0, 6), :]
         hold[i, pl.ds(8 + C, 6), :] = from_right[i, pl.ds(0, 6), :]
@@ -433,6 +432,9 @@
         hold[4 + i, pl.ds(8 + C, 4), :] = from_right[4 + i // 2, pl.ds(4 * (i % 2), 4), :]
         hold[8 + i, pl.ds(6, 2), :] = from_left[i, pl.ds(6, 2), :]
         hold[8 + i, pl.ds(8 + C, 2), :] = from_right[i, pl.ds(6, 2), :]
+    for copies in (halo_r, halo_t, edge_1[0]):
+        arrive(*copies)
+    sums()
     @pl.when(later)
     def _():
         for copy in cross_out[0]:
@@ -465,7 +467,7 @@
 
     def correct(i):
         src, dst = chain[i]
-        single(1, src, (), dst, rows_of(rf, i), edges)
+        single(1, src, (), dst, rows_of(rf, i), edges if i == 0 else [(first - 8, 40), (first + C - 32, 40)])
 
     def begin(i):
         for lo in (first - 8, first + C - 32):

time: 17.7 us -> 17.7 us (level)
  no operation moved by 1% of the time
where the time goes in v7:
time: 17.7 us; the launch traced here: 17.6 us
  Pallas kernels  16.3 us (92%)
  local copies, waits for them, and re-layouts  1.31 us (7%)
    pallas_call x1, Pallas kernels, local(): pl.pallas_call(kernel, out_shape=pltpu.VMEM(forcing.shape, F32), in_specs...  16.3 us
    transpose x1, local copies, waits for them, and re-layouts, local(): return jnp.swapaxes(by_column, 1, 2)  1.31 us

profile of v7, /device:TPU:132, one launch (start us, length us, event | category | flops | bytes accessed | tf_op | source)
XLA Modules:
  0.0 17.6 jit_solution(12774847133610201975)
XLA Ops:
  0.0 16.3 %shard_map.64 = f32[16,128,128]{2,1,0:T(8,128)S(1)} custom-call(f32[128,128]{1,0:T(8,128)} %u_hbm.1, f32[4,128,128]{2,1,0:T(8,128)} %guess_hbm.1, f32[16,128,128]{2,1,0:T(8,128)} %forcing_hbm.1, f32[128,128]{1,0:T(8,128)} %sx_hbm.1, f32[128,128]{1,0:T(8,128)} %sy_hbm.1, f32[128,128]{1,0:T(8,128)} %d_hbm.1), custom_call_target="tpu_custom_call" | custom-call | tf_op jit(solution)/shard_map/pallas_call | solution.py:554
  16.3 1.3 %copy.7 = f32[16,128,128]{2,1,0:T(8,128)} copy(f32[16,128,128]{1,2,0:T(8,128)S(1)} %bitcast.1) | data formatting | bytes 2097152 | tf_op jit(solution)/shard_map/transpose | solution.py:578
